TPU v7x, 128 devices: a whole 4x4x4 slice. The times are simulated.
128 devices in a mesh: tile: 64 (over z, y, x_hi, core), batch: 2 (over x_lo).
Axes of the slice: x: 4 (x_hi: 2, x_lo: 2; x = x_hi * 2 + x_lo), y: 4, z: 4, core: 2. Of those that a mesh axis runs over, the one named last changes fastest.
Arguments:
- fields: bfloat16 [2, 192, 32, 2048], P('batch', 'tile'), may hold values from -6 to 6
- cotangent: bfloat16 [2, 192, 32, 2048], P('batch', 'tile'), may hold values from -6 to 6
- first_kernel: float32 [3, 3, 64, 64], replicated, may hold values from -0.25 to 0.25
- second_kernel: float32 [3, 3, 64, 64], replicated, may hold values from -0.25 to 0.25
- adjacency: int32 [192, 4], replicated, may hold values from 0 to 191, as said below
- seam_codes: int32 [192, 4], replicated, may hold values from 0 to 7
- corner_map: int32 [192, 4], replicated, may hold values from 0 to 767, as said below
Outputs:
- output: bfloat16 [2, 192, 32, 2048], P('batch', 'tile')
- field_grad: bfloat16 [2, 192, 32, 2048], P('batch', 'tile')
- first_grad: float32 [3, 3, 64, 64], replicated
- second_grad: float32 [3, 3, 64, 64], replicated
Inputs may be any that keep to these rules, and one draw needn't show every extreme that they name: `adjacency`: tile t lies on device t // 3 of the tile axis; which sphere region each device holds is decided at run time, so the tables are data, not compile-time constants. Every edge of every tile meets exactly one edge of another tile, and mutually: if edge e of t meets edge e' of u then edge e' of u meets edge e of t with the same reversal. The edges joining one device's tiles to another device's tiles number at most 3, and some pair of devices reaches 3. `corner_map`: every entry names a corner pixel of a tile other than the tile itself.
All inputs are finite; a program needn't handle non-finite values.
Results may differ from a plain program's by a relative error of at most 0.0057.
Values may be sent and summed in bfloat16 or wider, within the bound.
A program may use at most 128 MiB of HBM per device.

v0:
```python
import math

import jax
import jax.numpy as jnp
from jax import lax
from jax.sharding import PartitionSpec as P

TILE_DEV = 3


def edge_strips(values):
    return jnp.stack(
        [values[..., -1, :, :], values[..., :, 0, :], values[..., 0, :, :], values[..., :, -1, :]],
        axis=-3,
    )


def corner_cells(values):
    return jnp.stack(
        [
            values[..., 0, 0, :],
            values[..., 0, -1, :],
            values[..., -1, 0, :],
            values[..., -1, -1, :],
        ],
        axis=-2,
    )


def framed(values, rim_vals, corner_vals):
    upper = jnp.concatenate(
        [corner_vals[..., 0:1, :], rim_vals[..., 2, :, :], corner_vals[..., 1:2, :]], axis=-2
    )
    lower = jnp.concatenate(
        [corner_vals[..., 2:3, :], rim_vals[..., 0, :, :], corner_vals[..., 3:4, :]], axis=-2
    )
    middle = jnp.concatenate(
        [rim_vals[..., 1, :, None, :], values, rim_vals[..., 3, :, None, :]], axis=-2
    )
    return jnp.concatenate([upper[..., None, :, :], middle, lower[..., None, :, :]], axis=-3)


def rim_parts(padded):
    interior = padded[..., 1:-1, 1:-1, :]
    rim_vals = jnp.stack(
        [
            padded[..., -1, 1:-1, :],
            padded[..., 1:-1, 0, :],
            padded[..., 0, 1:-1, :],
            padded[..., 1:-1, -1, :],
        ],
        axis=-3,
    )
    corner_vals = jnp.stack(
        [
            padded[..., 0, 0, :],
            padded[..., 0, -1, :],
            padded[..., -1, 0, :],
            padded[..., -1, -1, :],
        ],
        axis=-2,
    )
    return (interior, rim_vals, corner_vals)


def add_rims(interior, rim_vals, corner_vals):
    interior = interior.at[..., -1, :, :].add(rim_vals[..., 0, :, :])
    interior = interior.at[..., :, 0, :].add(rim_vals[..., 1, :, :])
    interior = interior.at[..., 0, :, :].add(rim_vals[..., 2, :, :])
    interior = interior.at[..., :, -1, :].add(rim_vals[..., 3, :, :])
    interior = interior.at[..., 0, 0, :].add(corner_vals[..., 0, :])
    interior = interior.at[..., 0, -1, :].add(corner_vals[..., 1, :])
    interior = interior.at[..., -1, 0, :].add(corner_vals[..., 2, :])
    interior = interior.at[..., -1, -1, :].add(corner_vals[..., 3, :])
    return interior


def conv_valid(padded, kernel):
    return lax.conv_general_dilated(
        padded,
        kernel,
        (1, 1),
        "VALID",
        dimension_numbers=("NHWC", "HWIO", "NHWC"),
        preferred_element_type=jnp.float32,
    )


def conv_full(tile_grad, kernel):
    turned = jnp.transpose(kernel[::-1, ::-1], (0, 1, 3, 2))
    return lax.conv_general_dilated(
        tile_grad,
        turned,
        (1, 1),
        ((2, 2), (2, 2)),
        dimension_numbers=("NHWC", "HWIO", "NHWC"),
        preferred_element_type=jnp.float32,
    )


def kernel_grad(padded, tile_grad):
    tile_side = tile_grad.shape[1]
    channels = tile_grad.shape[3]
    flat_grad = tile_grad.reshape(-1, channels)
    row_terms = []
    for shift_row in range(3):
        column_terms = []
        for shift_col in range(3):
            window = padded[
                :, shift_row : shift_row + tile_side, shift_col : shift_col + tile_side, :
            ].reshape(-1, channels)
            column_terms.append(
                lax.dot_general(
                    window, flat_grad, (((0,), (0,)), ((), ())), preferred_element_type=jnp.float32
                )
            )
        row_terms.append(jnp.stack(column_terms))
    return jnp.stack(row_terms)


def route_rims(strips, corner_vals, tables, backward):
    adjacency, seam_codes, corner_map = tables
    my_index = lax.axis_index("tile")
    my_tiles = my_index * TILE_DEV + jnp.arange(TILE_DEV, dtype=jnp.int32)
    slots = strips.shape[0]
    channels = corner_vals.shape[1]
    tile_side = strips.shape[1] // channels
    source_tile = adjacency[my_tiles].reshape(slots)
    source_edge = (seam_codes[my_tiles] % 4).reshape(slots)
    need_rows = source_tile * 4 + source_edge
    flat_map = corner_map.reshape(-1)
    if backward:
        corner_whole = flat_map
        corner_mine = my_index * slots + jnp.arange(slots, dtype=jnp.int32)
    else:
        corner_whole = jnp.arange(flat_map.shape[0], dtype=jnp.int32)
        corner_mine = corner_map[my_tiles].reshape(slots)
    pieces = (
        lax.all_gather(strips, "tile", axis=0, tiled=True),
        lax.all_gather(corner_vals, "tile", axis=0, tiled=True),
    )
    piece_rows = jnp.arange(pieces[0].shape[0], dtype=jnp.int32)
    strip_pick = (need_rows[:, None] == piece_rows[None, :]).astype(jnp.bfloat16)
    corner_pick = (corner_mine[:, None] == corner_whole[None, :]).astype(jnp.bfloat16)
    received = jnp.dot(strip_pick, pieces[0], preferred_element_type=jnp.float32)
    gathered_cells = jnp.dot(corner_pick, pieces[1], preferred_element_type=jnp.float32)
    flipped = (seam_codes[my_tiles] >= 4).reshape(slots)[:, None, None]
    shaped = received.reshape(slots, tile_side, channels)
    shaped = jnp.where(flipped, shaped[:, ::-1, :], shaped)
    return (
        shaped.reshape(TILE_DEV, 4, tile_side, channels),
        gathered_cells.reshape(TILE_DEV, 4, channels),
    )


def body(fields, cotangent, first_kernel, second_kernel, adjacency, seam_codes, corner_map):
    tile_local = fields.shape[1]
    tile_side = fields.shape[2]
    channels = first_kernel.shape[2]
    tables = (adjacency, seam_codes, corner_map)
    tile_field = fields.reshape(tile_local, tile_side, tile_side, channels)
    tile_grad = cotangent.reshape(tile_local, tile_side, tile_side, channels)
    w_first = first_kernel.astype(jnp.bfloat16)
    w_second = second_kernel.astype(jnp.bfloat16)

    def with_halo(values):
        strips = edge_strips(values).reshape(tile_local * 4, tile_side * channels)
        corner_vals = corner_cells(values).reshape(tile_local * 4, channels)
        rim_vals, gathered = route_rims(strips, corner_vals, tables, False)
        return framed(values, rim_vals.astype(jnp.bfloat16), gathered.astype(jnp.bfloat16))

    def adjoint(padded_grad):
        interior, rim_vals, corner_vals = rim_parts(padded_grad)
        strips = rim_vals.astype(jnp.bfloat16).reshape(tile_local * 4, tile_side * channels)
        cells_out = corner_vals.astype(jnp.bfloat16).reshape(tile_local * 4, channels)
        routed, summed = route_rims(strips, cells_out, tables, True)
        return add_rims(interior, routed, summed)

    padded_field = with_halo(tile_field)
    pre_act = conv_valid(padded_field, w_first)
    hidden = jax.nn.silu(pre_act).astype(jnp.bfloat16)
    padded_hidden = with_halo(hidden)
    output = (tile_field.astype(jnp.float32) + conv_valid(padded_hidden, w_second)).astype(
        jnp.bfloat16
    )
    second_grad = kernel_grad(padded_hidden, tile_grad)
    hidden_grad = adjoint(conv_full(tile_grad, w_second))
    sigmoid_pre = jax.nn.sigmoid(pre_act)
    pre_grad = (hidden_grad * sigmoid_pre * (1.0 + pre_act * (1.0 - sigmoid_pre))).astype(
        jnp.bfloat16
    )
    field_grad = (tile_grad.astype(jnp.float32) + adjoint(conv_full(pre_grad, w_first))).astype(
        jnp.bfloat16
    )
    first_grad = kernel_grad(padded_field, pre_grad)
    first_total, second_total = lax.psum((first_grad, second_grad), ("tile", "batch"))
    pixel_total = (
        lax.axis_size("batch") * lax.axis_size("tile") * tile_local * tile_side * tile_side
    )
    grad_scale = 1.0 / math.sqrt(pixel_total)
    shape_out = (1, tile_local, tile_side, tile_side * channels)
    return (
        output.reshape(shape_out),
        field_grad.reshape(shape_out),
        first_total * grad_scale,
        second_total * grad_scale,
    )


def solution(mesh):
    return jax.shard_map(
        body,
        mesh=mesh,
        in_specs=(
            P("batch", "tile", None, None),
            P("batch", "tile", None, None),
            P(),
            P(),
            P(),
            P(),
            P(),
        ),
        out_specs=(P("batch", "tile", None, None), P("batch", "tile", None, None), P(), P()),
        check_vma=False,
    )
```

profile of v0, /device:TPU:1, one launch (start us, length us, event | category | flops | bytes accessed | tf_op | source)
XLA Modules:
  0.0 690.4 jit_solution(5246875558716412720)
XLA Ops:
  7.2 1.9 reshape.746
  10.1 0.8 reshape.754
  12.4 3.9 fusion.95
  16.8 0.9 copy-done.13
  18.1 0.8 reshape.878
  21.4 99.7 %all-gather = bf16[64,12,64]{2,1,0:T(8,128)(2,1)S(1)} all-gather(bf16[1,12,64]{2,1,0:T(8,128)(2,1)S(1)} %reshape.870), channel_id=1, replica_groups=mesh['tile'=64,'batch'=2] {'tile'}, dimensions={0}, use_global_device_ids=true | all-gather | bytes 99840 | tf_op jit(solution)/shard_map/all_gather | solution.py:140
  121.5 2.0 copy.399
  123.7 1.3 copy-done.4
  126.1 89.9 %all-gather.5 = bf16[64,12,64]{2,1,0:T(8,128)(2,1)S(1)} all-gather(bf16[1,12,64]{2,1,0:T(8,128)(2,1)S(1)} %reshape.880), channel_id=1, replica_groups=mesh['tile'=64,'batch'=2] {'tile'}, dimensions={0}, use_global_device_ids=true | all-gather | bytes 99840 | tf_op jit(solution)/shard_map/all_gather | solution.py:140
  216.8 1.1 fusion.36
  219.3 6.2 reshape.873
  225.5 2.4 fusion.49
  230.6 1.6 fusion.4
  232.2 6.2 reshape.879
  238.4 2.4 fusion.47
  241.7 1.1 slice_add_fusion.3
  242.8 2.6 scatter-add.54
  245.4 0.8 fusion.45
  246.3 2.6 scatter-add.56
  248.9 0.8 fusion.43
  249.8 1.9 broadcast_select_fusion.3
  251.6 1.3 scatter-add.61
  253.4 5.0 add_divide_fusion
  259.2 1.0 copy-done.3
  262.0 3.9 fusion.96
  266.2 0.9 copy-done.14
  268.5 0.8 reshape_reshape.7
  269.3 2.6 reshape_reshape.6
  271.9 1.2 copy.425
  273.1 1.1 copy.383
  274.4 1.2 slice_bitcast_fusion.6
  275.6 1.2 copy.442
  277.7 92.7 %all-gather.2 = bf16[64,12,64]{2,1,0:T(8,128)(2,1)S(1)} all-gather(bf16[1,12,64]{2,1,0:T(8,128)(2,1)S(1)} %reshape.874), channel_id=1, replica_groups=mesh['tile'=64,'batch'=2] {'tile'}, dimensions={0}, use_global_device_ids=true | all-gather | bytes 99840 | tf_op jit(solution)/shard_map/all_gather | solution.py:140
  371.2 1.1 convolution_convert_fusion
  373.3 90.4 %all-gather.7 = bf16[64,12,64]{2,1,0:T(8,128)(2,1)S(1)} all-gather(bf16[1,12,64]{2,1,0:T(8,128)(2,1)S(1)} %reshape.884), channel_id=1, replica_groups=mesh['tile'=64,'batch'=2] {'tile'}, dimensions={0}, use_global_device_ids=true | all-gather | bytes 99840 | tf_op jit(solution)/shard_map/all_gather | solution.py:140
  464.4 1.1 fusion.34
  465.5 2.0 copy.413
  467.8 1.6 slice.919
  477.0 1.0 convolution_bitcast_fusion.4
  478.6 6.2 reshape.883
  484.8 2.4 fusion.46
  488.1 1.1 slice_add_fusion.1
  489.2 2.7 scatter-add.66
  491.9 1.5 fusion.41
  493.4 1.0 slice_add_fusion
  494.4 2.7 scatter-add.70
  497.2 1.4 fusion.39
  499.3 1.3 scatter-add.74
  500.6 2.6 broadcast_select_fusion.2
  503.2 2.6 scatter-add.75
  506.6 1.3 scatter-add.76
  507.9 3.5 copy.424
  512.1 6.3 reshape.877
  518.5 2.4 fusion.48
  522.2 1.5 maximum_bitcast_fusion.1
  529.9 1.4 scatter-add.79
  531.3 2.5 add_convert_fusion
  535.0 1.9 convolution_select_fusion.2
  538.8 1.9 fusion.10
  540.7 1.4 reshape.775
  542.1 2.5 reshape.753
  544.6 135.7 %all-reduce.3.cloned.1.call-done = (f32[3,3,64,64]{3,2,1,0:T(8,128)}, f32[3,3,64,64]{3,2,1,0:T(8,128)}) async-done(((f32[3,3,64,64]{3,2,1,0:T(8,128)}, f32[3,3,64,64]{3,2,1,0:T(8,128)}), (f32[3,3,64,64]{3,2,1,0:T(8,128)}, f32[3,3,64,64]{3,2,1,0:T(8,128)})) %all-reduce.3.cloned.1.call-update) | async-done | bytes 294928 | tf_op jit(solution)/shard_map/psum | solution.py:196
  680.3 1.7 broadcast_multiply_fusion
  682.0 1.7 broadcast_multiply_fusion.1
  (290 shorter events, 42.4 us)
Async XLA Ops:
  7.2 3.0 copy-start.11
  7.2 212.2 %all-gather.13.cloned.1.call-start = ((), (), s32[]{:S(2)}) async-start(), calls=%async_computation | async-start | bytes 4259840 | tf_op jit(solution)/shard_map/all_gather | solution.py:139
  10.1 222.1 %all-gather.17.cloned.1.call-start = ((), (), s32[]{:S(2)}) async-start(), calls=%async_computation.2 | async-start | bytes 4259840 | tf_op jit(solution)/shard_map/all_gather | solution.py:139
  11.4 1.0 copy-start.40
  11.4 1.0 copy-start.45
  16.5 2.4 copy-start.31
  16.5 2.5 copy-start.32
  16.5 4.0 copy-start.33
  16.7 1.0 copy-start.13
  18.9 459.8 %all-gather.19.cloned.1.call-start = ((), (), s32[]{:S(2)}) async-start(), calls=%async_computation.3 | async-start | bytes 4259840 | tf_op jit(solution)/shard_map/all_gather | solution.py:139
  19.3 197.5 %copy-start.34 = (s32[768]{0:T(1024)}, s32[768]{0:T(1024)S(1)}, u32[]{:S(2)}) copy-start(s32[768]{0:T(1024)S(1)} %eq.35) | copy-start | bytes 9220
  121.3 2.3 copy-start.36
  123.7 1.3 copy-start.4
  125.0 93.5 %copy-start.38 = (s32[4]{0:T(128)S(1)}, s32[4]{0:T(128)}, u32[]{:S(2)}) copy-start(s32[4]{0:T(128)} %constant.425.clone.1) | copy-start | bytes 52
  216.8 8.7 %copy-start.42 = (s32[12]{0:T(128)}, s32[12]{0:T(128)S(1)}, u32[]{:S(2)}) copy-start(s32[12]{0:T(128)S(1)} %iota_add_fusion) | copy-start | bytes 148
  228.3 0.6 copy-start.18
  228.4 0.6 copy-start.20
  228.4 0.6 copy-start.22
  229.0 0.6 copy-start.24
  241.0 0.7 copy-start.16
  253.4 5.0 copy-start.2
  258.8 1.4 copy-start.3
  260.7 11.2 %copy-start = (bf16[3,32,32,64]{3,1,2,0:T(8,128)(2,1)}, bf16[3,32,32,64]{3,1,2,0:T(8,128)(2,1)S(1)}, u32[]{:S(2)}) copy-start(bf16[3,32,32,64]{3,1,2,0:T(8,128)(2,1)S(1)} %fusion.7) | copy-start | bytes 1179652
  260.9 1.0 copy-start.39
  260.9 1.0 copy-start.46
  266.1 2.4 copy-start.12
  266.2 1.0 copy-start.14
  268.5 243.6 %all-gather.15.cloned.1.call-start = ((), (), s32[]{:S(2)}) async-start(), calls=%async_computation.1 | async-start | bytes 4259840 | tf_op jit(solution)/shard_map/all_gather | solution.py:139
  271.9 1.2 copy-start.15
  274.4 96.8 %copy-start.37 = (s32[12]{0:T(128)S(1)}, s32[12]{0:T(128)}, u32[]{:S(2)}) copy-start(s32[12]{0:T(128)} %copy-done.36) | copy-start | bytes 148
  275.6 188.8 %copy-start.35 = (s32[768]{0:T(1024)S(1)}, s32[768]{0:T(1024)}, u32[]{:S(2)}) copy-start(s32[768]{0:T(1024)} %copy-done.34) | copy-start | bytes 9220
  275.6 188.8 %copy-start.43 = (s32[12]{0:T(128)S(1)}, s32[12]{0:T(128)}, u32[]{:S(2)}) copy-start(s32[12]{0:T(128)} %copy-done.42) | copy-start | bytes 148
  373.2 307.1 %all-reduce.3.cloned.1.call-start = ((), (), s32[]{:S(2)}) async-start(), calls=%async_computation.4 | async-start | bytes 1179648 | tf_op jit(solution)/shard_map/psum | solution.py:196
  467.7 2.4 copy-start.5
  467.7 1.7 copy-start.19
  467.7 1.6 copy-start.21
  467.8 1.6 copy-start.23
  467.8 1.6 copy-start.25
  469.4 1.1 copy-start.1
  471.6 1.1 copy-start.8
  471.6 1.4 copy-start.9
  475.7 1.3 copy-start.7
  487.4 0.7 copy-start.17
  518.4 2.8 copy-start.29
  518.4 2.8 copy-start.30
  518.4 2.9 copy-start.27
  518.5 2.9 copy-start.28
  529.9 3.9 copy-start.6
  534.0 1.0 copy-start.41
  534.1 1.0 copy-start.44
  537.3 0.8 copy-start.26
  538.8 1.9 copy-start.10
Sparse Core Ops, SparseCore 0:
  11.8 75.9 all-gather.12
  91.6 70.1 all-gather.16
  268.6 68.7 all-gather.18
  373.3 66.0 all-gather.14
  539.0 141.3 all-reduce.2
where the time goes:
time: 699 us; the launch traced here: 690 us
  blocking collectives  373 us (53%)
  waiting for transfers between devices  136 us (19%)
  local copies, waits for them, and re-layouts  97.3 us (14%)
  matrix products  36.8 us (5%)
  other arithmetic  32.1 us (5%)
  between operations  15.5 us (2%)
    all_gather x4, blocking collectives, route_rims(): lax.all_gather(corner_vals, 'tile', axis=0, tiled=True)  373 us
    psum x1, waiting for transfers between devices, body(): lax.psum((first_grad, second_grad), ('tile', 'batch'))  136 us
    unnamed x129, local copies, waits for them, and re-layouts  41.6 us
  transfers between devices with their start and end apart: 5, of which 1 were waited for; matrix products, arithmetic and copies ran while one was open for 13% of the time, Pallas kernels for 0%

commit v1 on v0

v1 whole, which is shorter than its diff:
```python
import functools
import math

import jax
import jax.numpy as jnp
from jax import lax
from jax.experimental import pallas as pl
from jax.experimental.pallas import tpu as pltpu
from jax.sharding import PartitionSpec as P

TL = 3
S = 32
C = 64
NP = 16
R = TL * S
EDGES = TL * 4
LINES = EDGES * S
PARTS = EDGES + 1
PAIRS = NP + 2
PR = 128
MESH = pl.DeviceIdType.MESH
F32 = jnp.float32
BF = jnp.bfloat16
VM = pl.BlockSpec(memory_space=pltpu.VMEM)
SM = pl.BlockSpec(memory_space=pltpu.SMEM)


def rows_at(t):
    return t * 40 + 8


def low_lanes(rows):
    return lax.broadcasted_iota(jnp.int32, (rows, 128), 1) < C


def swap(v):
    return pltpu.roll(v, C, 1)


def put_lines(lines, first, second, place, out):
    low16, low32 = low_lanes(16), low_lanes(32)
    step = place(1, 0) - place(0, 0)
    for t in range(TL):
        for e, i in ((0, S - 1), (2, 0)):
            where = pl.ds(place(0, t) + i, NP, stride=step)
            a, b = first[where, :], second[where, :]
            base = (t * 4 + e) * S
            lines[pl.ds(base, NP, stride=2), :] = jnp.where(low16, a, swap(b))
            lines[pl.ds(base + 1, NP, stride=2), :] = jnp.where(low16, swap(a), b)
        for e, pair in ((1, 0), (3, NP - 1)):
            where = pl.ds(place(pair, t), S)
            a, b = first[where, :], second[where, :]
            line = jnp.where(low32, a, swap(b)) if e == 1 else jnp.where(low32, swap(a), b)
            lines[pl.ds((t * 4 + e) * S, S), :] = line
        for corner, (e, s) in enumerate(((2, 0), (2, S - 1), (0, 0), (0, S - 1))):
            lines[pl.ds(LINES + t * 4 + corner, 1), :] = lines[pl.ds((t * 4 + e) * S + s, 1), :]
    lines[pl.ds(LINES + EDGES, S - EDGES), :] = jnp.zeros((S - EDGES, 128), F32)
    for j in range(PARTS):
        out[j] = lines[pl.ds(j * S, S), :].astype(BF)


def fill_pad(pad, src):
    for p in (0, PAIRS - 1):
        pad[pl.ds(p * PR, PR), :] = jnp.zeros((PR, 128), F32)
    for p in range(NP):
        for t in range(TL):
            base = (p + 1) * PR + rows_at(t)
            pad[pl.ds(base - 8, 8), :] = jnp.zeros((8, 128), F32)
            pad[pl.ds(base, S), :] = src[t * S : (t + 1) * S, p * 128 : (p + 1) * 128].astype(F32)
        pad[pl.ds((p + 1) * PR + 120, 8), :] = jnp.zeros((8, 128), F32)


def pad_place(pair, t):
    return (pair + 1) * PR + rows_at(t)


def flat_place(pair, t):
    return pair * R + t * S


def make_shifts(xp, pad):
    for a in range(3):
        for p in range(PAIRS):
            for t in range(TL):
                xp[a, p, t * S : (t + 1) * S, :] = pad[pl.ds(p * PR + rows_at(t) - 1 + a, S), :].astype(BF)


def build_forward(w_out, w):
    w_out[...] = jnp.zeros_like(w_out)
    for a in range(3):
        for c in range(3):
            block = w[a, c].astype(BF)
            for n in range(4):
                m = n + 1 + c
                w_out[a, m * C : (m + 1) * C, n * C : (n + 1) * C] = block


def build_backward(w_out, w_rim, w_corner, w):
    w_out[...] = jnp.zeros_like(w_out)
    w_rim[...] = jnp.zeros_like(w_rim)
    w_corner[...] = jnp.zeros_like(w_corner)
    for a in range(3):
        for c in range(3):
            block = w[a, c].T.astype(BF)
            for n in range(4):
                m = n + 3 - c
                w_out[2 - a, m * C : (m + 1) * C, n * C : (n + 1) * C] = block
            spots = []
            if a == 2:
                spots.append((0, c))
            if c == 0:
                spots.append((1, a))
            if a == 0:
                spots.append((2, c))
            if c == 2:
                spots.append((3, a))
            for e, tap in spots:
                w_rim[tap * 128 + C : tap * 128 + 128, e * C : (e + 1) * C] = block
            if a != 1 and c != 1:
                corner = (a // 2) * 2 + c // 2
                w_corner[C:128, corner * C : (corner + 1) * C] = block


def conv(xp, w):
    total = None
    for a in range(3):
        left = jnp.concatenate(
            [
                jnp.concatenate([xp[a, 2 * q + s] for q in range(NP // 2)], axis=0)
                for s in range(4)
            ],
            axis=1,
        )
        part = jnp.dot(left, w[a], preferred_element_type=F32)
        total = part if total is None else total + part
    return total


def kernel_grad(xp, q, a, upper):
    wide = jnp.concatenate(
        [jnp.concatenate([xp[a, d + p] for p in range(NP)], axis=0) for d in range(3)], axis=1
    )
    out = lax.dot_general(q, wide, (((0,), (0,)), ((), ())), preferred_element_type=F32)
    turned = jnp.concatenate([out[:, d * 128 : (d + 1) * 128].T for d in range(3)], axis=0)
    here, there = turned[64:256], turned[128:320]
    return swap(here) + there if upper else here + swap(there)


def orient(lines_ref, tab, me, w_rim, turned):
    lines = lines_ref[...].astype(F32)
    low = low_lanes(S)
    spot = lax.broadcasted_iota(jnp.int32, (LINES, 128), 0) % S
    after = jnp.where(spot == S - 1, 0.0, pltpu.roll(lines, LINES - 1, 0)).astype(BF)
    before = jnp.where(spot == 0, 0.0, pltpu.roll(lines, 1, 0)).astype(BF)
    wide = jnp.concatenate([after, lines_ref[...], before], axis=1)
    rims = jnp.dot(wide, w_rim[...], preferred_element_type=F32)
    flip = (
        lax.broadcasted_iota(jnp.int32, (S, S), 0) + lax.broadcasted_iota(jnp.int32, (S, S), 1)
        == S - 1
    )
    flip = jnp.where(flip, 1.0, 0.0).astype(BF)
    kept = []
    codes = [tab[768 + me * EDGES + j] for j in range(EDGES)]
    for j in range(EDGES):
        e = codes[j] % 4
        at = slice(j * S, (j + 1) * S)
        pair = jnp.where(e >= 2, rims[at, 128:], rims[at, :128])
        rim = jnp.where(e % 2 == 1, pair, swap(pair))
        kept.append(jnp.where(low, lines[at], rim).astype(BF))
    flipped = jnp.dot(flip, jnp.concatenate(kept, axis=1), preferred_element_type=F32)
    for j in range(EDGES):
        turned[pl.ds(j * S, S), :] = jnp.where(
            codes[j] >= 4, flipped[:, j * 128 : (j + 1) * 128], kept[j].astype(F32)
        )


def halo_in(pad, turned, cells):
    low16 = low_lanes(16)
    cells_swapped = swap(cells[...])
    for t in range(TL):
        for e, row in ((0, rows_at(t) + S), (2, rows_at(t) - 1)):
            base = (t * 4 + e) * S
            even = turned[pl.ds(base, NP, stride=2), :]
            odd = turned[pl.ds(base + 1, NP, stride=2), :]
            pad[pl.ds(PR + row, NP, stride=PR), :] = jnp.where(low16, even, swap(odd))
        pad[pl.ds(rows_at(t), S), :] = swap(turned[pl.ds((t * 4 + 1) * S, S), :])
        pad[pl.ds((PAIRS - 1) * PR + rows_at(t), S), :] = turned[pl.ds((t * 4 + 3) * S, S), :]
        for corner, (row, p) in enumerate(((-1, 0), (-1, 1), (S, 0), (S, 1))):
            at = t * 4 + corner
            value = (cells[...] if p else cells_swapped)[at : at + 1]
            pad[pl.ds(p * (PAIRS - 1) * PR + rows_at(t) + row, 1), :] = value


def corner_sums(corners_ref, corner_row, me, w_corner):
    every = jnp.dot(corners_ref[...], w_corner[...], preferred_element_type=F32)
    kind = lax.broadcasted_iota(jnp.int32, (1024, 128), 0) % 4
    pair = jnp.where(kind >= 2, every[:, 128:], every[:, :128])
    other = swap(pair)
    low = low_lanes(1024)
    both = jnp.where((kind % 2 == 1) == low, other, pair).astype(BF)
    mine = me * EDGES + lax.broadcasted_iota(jnp.int32, (16, 1024), 0)
    real = lax.broadcasted_iota(jnp.int32, (16, 1024), 0) < EDGES
    pick = jnp.where((corner_row[...] == mine) & real, 1.0, 0.0).astype(BF)
    return jnp.dot(pick, both, preferred_element_type=F32)


def rims_in(back, turned, sums):
    low16, low32, low1 = low_lanes(16), low_lanes(S), low_lanes(16)
    for t in range(TL):
        for e, i in ((0, S - 1), (2, 0)):
            base = (t * 4 + e) * S
            even = turned[pl.ds(base, NP, stride=2), :]
            odd = turned[pl.ds(base + 1, NP, stride=2), :]
            at = pl.ds(t * S + i, NP, stride=R)
            back[at, :] = back[at, :] + jnp.where(low16, swap(even), odd)
        at = pl.ds(t * S, S)
        line = swap(turned[pl.ds((t * 4 + 1) * S, S), :])
        back[at, :] = back[at, :] + jnp.where(low32, line, 0.0)
        at = pl.ds((NP - 1) * R + t * S, S)
        back[at, :] = back[at, :] + jnp.where(low32, 0.0, turned[pl.ds((t * 4 + 3) * S, S), :])
    lows, highs = jnp.where(low1, sums, 0.0), jnp.where(low1, 0.0, sums)
    for t in range(TL):
        for corner, (i, p) in enumerate(((0, 0), (0, 1), (S - 1, 0), (S - 1, 1))):
            at = pl.ds(p * (NP - 1) * R + t * S + i, 1)
            s = t * 4 + corner
            back[at, :] = back[at, :] + (highs if p else lows)[s : s + 1]


def both_convs(
    x_ref, q_ref, wf_ref, wb_ref, lines_ref, corners_ref, corner_row, tab,
    pad, xp, qp, w_conv, w_rim, w_corner, turned, cells_all, cells, main, back,
):
    me = lax.axis_index("tile")
    build_backward(w_conv, w_rim, w_corner, wb_ref)
    fill_pad(pad, q_ref)
    make_shifts(qp, pad)
    out = conv(qp, w_conv)
    for q in range(NP // 2):
        for half in range(2):
            back[pl.ds((2 * q + half) * R, R), :] = out[q * R : (q + 1) * R, half * 128 : (half + 1) * 128]
    orient(lines_ref, tab, me, w_rim, turned)
    sums = corner_sums(corners_ref, corner_row, me, w_corner)
    rims_in(back, turned, sums)
    cells_all[...] = corners_ref[...].astype(F32)
    for s in range(EDGES):
        v = tab[1536 + me * EDGES + s]
        tile = v // 4
        device = tile // 3
        row = device * 16 + (tile - device * 3) * 4 + v % 4
        cells[pl.ds(s, 1), :] = cells_all[pl.ds(row, 1), :]
    cells[pl.ds(EDGES, 4), :] = jnp.zeros((4, 128), F32)
    fill_pad(pad, x_ref)
    halo_in(pad, turned, cells)
    make_shifts(xp, pad)
    build_forward(w_conv, wf_ref)
    main[...] = conv(xp, w_conv)


CONV_SCRATCH = [
    pltpu.VMEM((PAIRS * PR, 128), F32),
    pltpu.VMEM((3, PAIRS, R, 128), BF),
    pltpu.VMEM((3, PAIRS, R, 128), BF),
    pltpu.VMEM((3, 512, 256), BF),
    pltpu.VMEM((384, 256), BF),
    pltpu.VMEM((128, 256), BF),
    pltpu.VMEM((LINES, 128), F32),
    pltpu.VMEM((1024, 128), F32),
    pltpu.VMEM((16, 128), F32),
    pltpu.VMEM((NP // 2 * R, 256), F32),
    pltpu.VMEM((NP * R, 128), F32),
]


def start_kernel(f_ref, c_ref, out, pad_a, pad_b, lines):
    fill_pad(pad_a, f_ref)
    fill_pad(pad_b, c_ref)
    put_lines(lines, pad_a, pad_b, pad_place, out)


def middle_kernel(
    f_ref, c_ref, w1_ref, w2_ref, lines_ref, corners_ref, corner_row, tab,
    hidden, pre_grad, grad, out,
    pad, xp, qp, w_conv, w_rim, w_corner, turned, cells_all, cells, main, back, hid, lines, grads,
):
    both_convs(
        f_ref, c_ref, w1_ref, w2_ref, lines_ref, corners_ref, corner_row, tab,
        pad, xp, qp, w_conv, w_rim, w_corner, turned, cells_all, cells, main, back,
    )
    for p in range(NP):
        pre = main[pl.ds((p // 2) * R, R), (p % 2) * 128 : (p % 2) * 128 + 128]
        at = pl.ds(p * R, R)
        s = 1.0 / (1.0 + jnp.exp(-pre))
        h = (pre * s).astype(BF)
        g = (back[at, :] * s * (1.0 + pre * (1.0 - s))).astype(BF)
        hidden[:, p * 128 : (p + 1) * 128] = h
        pre_grad[:, p * 128 : (p + 1) * 128] = g
        hid[at, :] = h.astype(F32)
        back[at, :] = g.astype(F32)
        grads[at, :] = g
    put_lines(lines, hid, back, flat_place, out)
    for a in range(3):
        grad[pl.ds(a * 192, 192), :] = kernel_grad(xp, grads[...], a, False)


def last_kernel(
    h_ref, g_ref, f_ref, c_ref, w1_ref, w2_ref, lines_ref, corners_ref, corner_row, tab, grad_one,
    output, field_grad, grad,
    pad, xp, qp, w_conv, w_rim, w_corner, turned, cells_all, cells, main, back, grads,
):
    both_convs(
        h_ref, g_ref, w2_ref, w1_ref, lines_ref, corners_ref, corner_row, tab,
        pad, xp, qp, w_conv, w_rim, w_corner, turned, cells_all, cells, main, back,
    )
    for p in range(NP):
        at, lanes = pl.ds(p * R, R), slice(p * 128, (p + 1) * 128)
        made = main[pl.ds((p // 2) * R, R), (p % 2) * 128 : (p % 2) * 128 + 128]
        output[:, lanes] = (f_ref[:, lanes].astype(F32) + made).astype(BF)
        c = c_ref[:, lanes]
        field_grad[:, lanes] = (c.astype(F32) + back[at, :]).astype(BF)
        grads[at, :] = c
    low = low_lanes(192)
    for a in range(3):
        at = pl.ds(a * 192, 192)
        grad[at, :] = jnp.where(low, grad_one[at, :], kernel_grad(xp, grads[...], a, True))


def exchange_kernel(x_ref, tab, out_lines, out_corners, held, stage, got, s_z, r_z, s_c, r_c, s_p, r_p):
    t = lax.axis_index("tile")
    b = lax.axis_index("batch")
    z, plane, core = t // 16, (t // 2) % 8, t % 2

    def device(z, plane, core):
        return (z * 16 + plane * 2 + core, b)

    partners = [device((z + k) % 4, plane, core) for k in range(1, 4)]
    partners.append(device(z, plane, 1 - core))
    partners += [device(z, (plane + k) % 8, core) for k in range(1, 8)]
    barrier = pltpu.get_barrier_semaphore()
    for other in partners:
        pl.semaphore_signal(barrier, inc=1, device_id=other, device_id_type=MESH)
    pl.semaphore_wait(barrier, len(partners))

    def slot(z, core):
        return held.at[pl.ds((z * 2 + core) * PARTS, PARTS)]

    def remote(src, dst, send, recv, other):
        copy = pltpu.make_async_remote_copy(
            src_ref=src, dst_ref=dst, send_sem=send, recv_sem=recv, device_id=other, device_id_type=MESH
        )
        copy.start()
        return copy

    along = [remote(x_ref, slot(z, core), s_z.at[k], r_z.at[k], partners[k]) for k in range(3)]
    across = [remote(x_ref, slot(z, core), s_c.at[0], r_c.at[0], partners[3])]
    held[pl.ds((z * 2 + core) * PARTS, PARTS)] = x_ref[...]
    for k in range(3):
        along[k].wait_recv()
        here = slot((z + 3 - k) % 4, core)
        across.append(remote(here, here, s_c.at[k + 1], r_c.at[k + 1], partners[3]))
    for copy in across:
        copy.wait_recv()

    def entry(dev, j):
        tile, code = tab[dev * EDGES + j], tab[768 + dev * EDGES + j]
        source = (tile * 171) >> 9
        return source, (tile - source * 3) * 4 + (code & 3)

    planes = []
    for k in range(8):
        other = (plane + k) % 8

        def take(j, _, k=k, other=other):
            source, line = entry(z * 16 + other * 2 + core, j)
            stage[k, j] = held[((source >> 4) * 2 + (source & 1)) * PARTS + line]
            return 0

        lax.fori_loop(0, EDGES, take, 0)
        for s in range(8):
            stage[k, EDGES + s // 2, (s % 2) * 16 : (s % 2) * 16 + 16, :] = held[s * PARTS + EDGES, :16, :]
        if k:
            planes.append(
                remote(stage.at[k], got.at[pl.ds(plane * 16, 16)], s_p.at[k - 1], r_p.at[k - 1], partners[3 + k])
            )
        else:
            got[pl.ds(plane * 16, 16)] = stage[0]
    for copy in planes:
        copy.wait_recv()

    def give(j, _):
        source, _line = entry(t, j)
        out_lines[pl.ds(pl.multiple_of(j * S, S), S), :] = got[((source >> 1) & 7) * 16 + j]
        return 0

    lax.fori_loop(0, EDGES, give, 0)
    for zz in range(4):
        for pp in range(8):
            out_corners[(zz * 8 + pp) * 32 : (zz * 8 + pp) * 32 + 32, :] = got[pp * 16 + EDGES + zz]
    for copy in along + across + planes:
        copy.wait_send()


def exchange(lines, tab, ident):
    sem = pltpu.SemaphoreType.DMA
    return pl.pallas_call(
        exchange_kernel,
        out_shape=(jax.ShapeDtypeStruct((LINES, 128), BF), jax.ShapeDtypeStruct((1024, 128), BF)),
        in_specs=[VM, SM],
        out_specs=(VM, VM),
        scratch_shapes=[
            pltpu.VMEM((8 * PARTS, S, 128), BF),
            pltpu.VMEM((8, 16, S, 128), BF),
            pltpu.VMEM((8 * 16, S, 128), BF),
            sem((3,)), sem((3,)), sem((4,)), sem((4,)), sem((7,)), sem((7,)),
        ],
        name="exchange",
        compiler_params=pltpu.CompilerParams(
            collective_id=ident, has_side_effects=True, vmem_limit_bytes=40 * 2**20
        ),
    )(lines, tab)


def total_kernel(x_ref, out, mine, parts, ys, zs, s_a, r_a, s_y, r_y, s_z, r_z, s_g, r_g):
    t = lax.axis_index("tile")
    b = lax.axis_index("batch")
    z, y, hi, core = t // 16, (t // 4) % 4, (t // 2) % 2, t % 2
    group = hi * 4 + b * 2 + core
    rows = 72

    def device(z, y, g):
        return (z * 16 + y * 4 + (g // 4) * 2 + g % 2, (g // 2) % 2)

    near = [device(z, y, (group + k) % 8) for k in range(1, 8)]
    along_y = [device(z, (y + k) % 4, group) for k in range(1, 4)]
    along_z = [device((z + k) % 4, y, group) for k in range(1, 4)]
    barrier = pltpu.get_barrier_semaphore()
    for other in near + along_y + along_z:
        pl.semaphore_signal(barrier, inc=1, device_id=other, device_id_type=MESH)
    pl.semaphore_wait(barrier, 13)

    def remote(src, dst, send, recv, other):
        copy = pltpu.make_async_remote_copy(
            src_ref=src, dst_ref=dst, send_sem=send, recv_sem=recv, device_id=other, device_id_type=MESH
        )
        copy.start()
        return copy

    def piece(ref, g):
        return ref.at[pl.ds(pl.multiple_of(g * rows, 8), rows)]

    copies = [
        remote(piece(x_ref, (group + k) % 8), parts.at[group], s_a.at[k - 1], r_a.at[k - 1], near[k - 1])
        for k in range(1, 8)
    ]
    parts[group] = x_ref[pl.ds(pl.multiple_of(group * rows, 8), rows), :]
    for copy in copies:
        copy.wait_recv()
    total = parts[0]
    for g in range(1, 8):
        total = total + parts[g]
    for ref, me, others, send, recv in ((ys, y, along_y, s_y, r_y), (zs, z, along_z, s_z, r_z)):
        ref[me] = total
        step = [remote(ref.at[me], ref.at[me], send.at[k], recv.at[k], others[k]) for k in range(3)]
        for copy in step:
            copy.wait_recv()
        total = ((ref[0] + ref[1]) + ref[2]) + ref[3]
        copies += step
    mine[...] = total
    last = [remote(mine, piece(out, group), s_g.at[k], r_g.at[k], near[k]) for k in range(7)]
    out[pl.ds(pl.multiple_of(group * rows, 8), rows), :] = total
    for copy in last:
        copy.wait_recv()
    for copy in copies + last:
        copy.wait_send()


def total(x, ident):
    sem = pltpu.SemaphoreType.DMA
    return pl.pallas_call(
        total_kernel,
        out_shape=jax.ShapeDtypeStruct((576, 128), F32),
        in_specs=[VM],
        out_specs=VM,
        scratch_shapes=[
            pltpu.VMEM((72, 128), F32),
            pltpu.VMEM((8, 72, 128), F32),
            pltpu.VMEM((4, 72, 128), F32),
            pltpu.VMEM((4, 72, 128), F32),
            sem((7,)), sem((7,)), sem((3,)), sem((3,)), sem((3,)), sem((3,)), sem((7,)), sem((7,)),
        ],
        name="total",
        compiler_params=pltpu.CompilerParams(collective_id=ident, has_side_effects=True),
    )(x)


def body(fields, cotangent, first_kernel, second_kernel, adjacency, seam_codes, corner_map):
    f = fields.reshape(R, S * C)
    c = cotangent.reshape(R, S * C)
    tab = jnp.concatenate([adjacency.reshape(-1), seam_codes.reshape(-1), corner_map.reshape(-1)])
    corner_row = jnp.pad(corner_map.reshape(64, EDGES), ((0, 0), (0, 4)), constant_values=-1)
    corner_row = corner_row.reshape(1, 1024)
    wide = jax.ShapeDtypeStruct((R, S * C), BF)
    sent = jax.ShapeDtypeStruct((PARTS, S, 128), BF)
    sums = jax.ShapeDtypeStruct((576, 128), F32)
    params = pltpu.CompilerParams(vmem_limit_bytes=48 * 2**20)

    lines = pl.pallas_call(
        start_kernel,
        out_shape=sent,
        in_specs=[VM, VM],
        out_specs=VM,
        scratch_shapes=[
            pltpu.VMEM((PAIRS * PR, 128), F32),
            pltpu.VMEM((PAIRS * PR, 128), F32),
            pltpu.VMEM((PARTS * S, 128), F32),
        ],
        name="lines",
        compiler_params=params,
    )(f, c)
    near, cells = exchange(lines, tab, 0)
    hidden, pre_grad, grad_one, lines = pl.pallas_call(
        middle_kernel,
        out_shape=(wide, wide, sums, sent),
        in_specs=[VM] * 7 + [SM],
        out_specs=(VM,) * 4,
        scratch_shapes=CONV_SCRATCH
        + [
            pltpu.VMEM((NP * R, 128), F32),
            pltpu.VMEM((PARTS * S, 128), F32),
            pltpu.VMEM((NP * R, 128), BF),
        ],
        name="middle",
        compiler_params=params,
    )(f, c, first_kernel, second_kernel, near, cells, corner_row, tab)
    near, cells = exchange(lines, tab, 1)
    output, field_grad, grads = pl.pallas_call(
        last_kernel,
        out_shape=(wide, wide, sums),
        in_specs=[VM] * 9 + [SM, VM],
        out_specs=(VM,) * 3,
        scratch_shapes=CONV_SCRATCH + [pltpu.VMEM((NP * R, 128), BF)],
        name="last",
        compiler_params=params,
    )(hidden, pre_grad, f, c, first_kernel, second_kernel, near, cells, corner_row, tab, grad_one)
    grads = total(grads, 2)
    grad_scale = 1.0 / math.sqrt(2 * 192 * S * S)
    shape_out = (1, TL, S, S * C)
    return (
        output.reshape(shape_out),
        field_grad.reshape(shape_out),
        grads[:, :C].reshape(3, 3, C, C) * grad_scale,
        grads[:, C:].reshape(3, 3, C, C) * grad_scale,
    )


def solution(mesh):
    split = P("batch", "tile", None, None)
    return jax.shard_map(
        body,
        mesh=mesh,
        in_specs=(split, split, P(), P(), P(), P(), P()),
        out_specs=(split, split, P(), P()),
        check_vma=False,
    )
```

time: 699 us -> 99 us (0.14); the launches traced: 690 us -> 98.8 us
  blocking collectives: 373 us -> 0 us
  waiting for transfers between devices: 136 us -> 0 us
  local copies, waits for them, and re-layouts: 97.3 us -> 2.53 us
  Pallas kernels: 0 us -> 93.5 us
  matrix products: 36.8 us -> 0 us
  other arithmetic: 32.1 us -> 1.95 us
  between operations: 15.5 us -> 0.82 us
    all_gather x4 -> x0, blocking collectives: 373 us -> none  [route_rims(): lax.all_gather(corner_vals, 'tile', axis=0, tiled=True)]
    psum x1 -> x0, waiting for transfers between devices: 136 us -> none  [body(): lax.psum((first_grad, second_grad), ('tile', 'batch'))]
    pallas_call x0 -> x6, Pallas kernels: none -> 93.5 us  [the longest x2 59.1 us: exchange(): pl.pallas_call(exchange_kernel, out_shape=(jax.ShapeDtypeStruct((LINES, 1...]
    unnamed x129 -> x21, local copies, waits for them, and re-layouts: 41.6 us -> 2.03 us
    scatter-add x13 -> x0, local copies, waits for them, and re-layouts: 22.6 us -> none  [the longest x2 5.34 us: add_rims(): interior = interior.at[..., 0, :, :].add(rim_vals[..., 2, :, :])]
    dot_general x26 -> x0, matrix products: 22.1 us -> none  [the longest x4 9.78 us: route_rims(): jnp.dot(strip_pick, pieces[0], preferred_element_type=jnp.float32)]
    conv_general_dilated x4 -> x0, matrix products: 14.7 us -> none  [the longest x2 7.88 us: conv_full(): lax.conv_general_dilated(tile_grad, turned, (1, 1), ((2, 2), (2, 2)), dim...]
    another operation x20 -> x0, other arithmetic: 7.43 us -> none
  transfers between devices with their start and end apart: 5 -> 0, of which waited for: 1 -> 0; matrix products, arithmetic and copies ran while one was open for 13% -> 0% of each run, Pallas kernels for 0% -> 0%
where the time goes in v1:
time: 99 us; the launch traced here: 98.8 us
  Pallas kernels  93.5 us (94%)
  local copies, waits for them, and re-layouts  2.53 us (3%)
  other arithmetic  1.95 us (2%)
    pallas_call x2, Pallas kernels, exchange(): pl.pallas_call(exchange_kernel, out_shape=(jax.ShapeDtypeStruct((LINES, 1...  59.1 us
    pallas_call x1, Pallas kernels, total(): pl.pallas_call(total_kernel, out_shape=jax.ShapeDtypeStruct((576, 128), F...  24.7 us
    pallas_call x1, Pallas kernels, body(): pl.pallas_call(middle_kernel, out_shape=(wide, wide, sums, sent), in_spec...  5.06 us
    pallas_call x1, Pallas kernels, body(): pl.pallas_call(last_kernel, out_shape=(wide, wide, sums), in_specs=[VM] *...  4.42 us
    unnamed x21, local copies, waits for them, and re-layouts  2.03 us

profile of v1, /device:TPU:1, one launch (start us, length us, event | category | flops | bytes accessed | tf_op | source)
XLA Modules:
  0.0 98.8 jit_solution(1094826091860279831)
XLA Ops:
  0.6 0.0 copy-start.5
  0.6 0.7 copy-done.5
  1.3 0.0 copy-start.6
  1.3 0.0 copy-start.7
  1.3 0.0 copy-start.1
  1.3 0.1 copy.13
  1.4 0.0 copy-start
  1.5 0.1 reshape.45
  1.6 0.1 reshape.46
  1.7 0.1 reshape.47.corner_row
  1.7 0.3 copy-done.6
  2.0 0.1 copy.11
  2.1 0.1 reshape.43
  2.3 0.0 copy-done.7
  2.3 0.1 copy.12
  2.4 0.1 reshape.44
  2.5 0.0 copy-done.1
  2.5 0.0 copy-done
  2.6 0.0 copy-start.2
  2.6 0.0 copy-start.3
  2.6 0.2 lines.1.x_ref
  2.8 31.4 %exchange.2 = (bf16[384,128]{1,0:T(8,128)(2,1)S(1)}, bf16[1024,128]{1,0:T(8,128)(2,1)S(1)}) custom-call(bf16[13,32,128]{2,1,0:T(8,128)(2,1)S(1)} %lines.1.x_ref, s32[2304]{0:T(1024)S(1)} %constant_dynamic-update-slice_fusion.tab), custom_call_target="tpu_custom_call" | custom-call | tf_op jit(solution)/shard_map/exchange/pallas_call | solution.py:404
  34.3 0.0 copy-done.2
  34.3 0.0 copy-done.3
  34.3 5.1 %middle.1 = (bf16[96,2048]{1,0:T(8,128)(2,1)S(1)}, bf16[96,2048]{1,0:T(8,128)(2,1)S(1)}, f32[576,128]{1,0:T(8,128)S(1)}, bf16[13,32,128]{2,1,0:T(8,128)(2,1)S(1)}) custom-call(bf16[96,2048]{1,0:T(8,128)(2,1)S(1)} %bitcast.7, bf16[96,2048]{1,0:T(8,128)(2,1)S(1)} %bitcast.10, f32[3,3,64,64]{3,2,1,0:T(8,128)S(1)} %copy-done.2, f32[3,3,64,64]{3,2,1,0:T(8,128)S(1)} %copy-done.3, ...), custom_call_target="tpu_custom_call" | custom-call | tf_op jit(solution)/shard_map/middle/pallas_call | solution.py:520
  39.4 27.6 %exchange.3 = (bf16[384,128]{1,0:T(8,128)(2,1)S(1)}, bf16[1024,128]{1,0:T(8,128)(2,1)S(1)}) custom-call(bf16[13,32,128]{2,1,0:T(8,128)(2,1)S(1)} %get-tuple-element.19.x_ref, s32[2304]{0:T(1024)S(1)} %constant_dynamic-update-slice_fusion.tab), custom_call_target="tpu_custom_call" | custom-call | tf_op jit(solution)/shard_map/exchange/pallas_call | solution.py:404
  67.0 4.4 %last.1 = (bf16[96,2048]{1,0:T(8,128)(2,1)}, bf16[96,2048]{1,0:T(8,128)(2,1)}, f32[576,128]{1,0:T(8,128)S(1)}) custom-call(bf16[96,2048]{1,0:T(8,128)(2,1)S(1)} %get-tuple-element.17.h_ref, bf16[96,2048]{1,0:T(8,128)(2,1)S(1)} %get-tuple-element.18.g_ref, bf16[96,2048]{1,0:T(8,128)(2,1)S(1)} %bitcast.8, bf16[96,2048]{1,0:T(8,128)(2,1)S(1)} %bitcast.11, ...), custom_call_target="tpu_custom_call" | custom-call | tf_op jit(solution)/shard_map/last/pallas_call | solution.py:535
  71.4 0.0 copy-start.4
  71.4 0.7 copy-done.4
  72.1 24.7 %total.1 = f32[576,128]{1,0:T(8,128)} custom-call(f32[576,128]{1,0:T(8,128)} %copy-done.4), custom_call_target="tpu_custom_call" | custom-call | tf_op jit(solution)/shard_map/total/pallas_call | solution.py:478
  96.8 2.0 %slice_multiply_fusion = (f32[576,64]{1,0:T(8,128)}, f32[576,64]{1,0:T(8,128)}) fusion(f32[576,128]{1,0:T(8,128)} %total.1), kind=kLoop, calls=%fused_computation | loop fusion | flops 73728 | bytes 589824 | tf_op jit(solution)/shard_map/mul | solution.py:551
  (5 shorter events, 0.0 us)
Async XLA Ops:
  0.6 0.7 copy-start.5
  1.3 0.7 copy-start.6
  1.3 0.9 copy-start.7
  1.3 1.2 %copy-start.1 = (bf16[1,3,32,2048]{3,2,1,0:T(8,128)(2,1)S(1)}, bf16[1,3,32,2048]{3,2,1,0:T(8,128)(2,1)}, u32[]{:S(2)}) copy-start(bf16[1,3,32,2048]{3,2,1,0:T(8,128)(2,1)} %param.8) | copy-start | bytes 1179652
  1.4 1.1 %copy-start = (bf16[1,3,32,2048]{3,2,1,0:T(8,128)(2,1)S(1)}, bf16[1,3,32,2048]{3,2,1,0:T(8,128)(2,1)}, u32[]{:S(2)}) copy-start(bf16[1,3,32,2048]{3,2,1,0:T(8,128)(2,1)} %param.7) | copy-start | bytes 1179652
  2.6 31.7 %copy-start.2 = (f32[3,3,64,64]{3,2,1,0:T(8,128)S(1)}, f32[3,3,64,64]{3,2,1,0:T(8,128)}, u32[]{:S(2)}) copy-start(f32[3,3,64,64]{3,2,1,0:T(8,128)} %w1_ref.3) | copy-start | bytes 442372
  2.6 31.7 %copy-start.3 = (f32[3,3,64,64]{3,2,1,0:T(8,128)S(1)}, f32[3,3,64,64]{3,2,1,0:T(8,128)}, u32[]{:S(2)}) copy-start(f32[3,3,64,64]{3,2,1,0:T(8,128)} %w2_ref.3) | copy-start | bytes 442372
  71.4 0.7 copy-start.4

commit v2 on v1

v2 whole, which is shorter than its diff:
```python
import functools
import math

import jax
import jax.numpy as jnp
from jax import lax
from jax.experimental import pallas as pl
from jax.experimental.pallas import tpu as pltpu
from jax.sharding import PartitionSpec as P

TL = 3
S = 32
C = 64
NP = 16
R = TL * S
EDGES = TL * 4
LINES = EDGES * S
HALF = S // 2
SHARE = 9 * C // 8
PAIRS = NP + 2
PR = 128
MESH = pl.DeviceIdType.MESH
F32 = jnp.float32
BF = jnp.bfloat16
VM = pl.BlockSpec(memory_space=pltpu.VMEM)
SM = pl.BlockSpec(memory_space=pltpu.SMEM)


def rows_at(t):
    return t * 40 + 8


def low_lanes(rows):
    return lax.broadcasted_iota(jnp.int32, (rows, 128), 1) < C


def swap(v):
    return pltpu.roll(v, C, 1)


def put_lines(lines, first, second, place, out):
    low16, low32 = low_lanes(16), low_lanes(32)
    step = place(1, 0) - place(0, 0)
    for t in range(TL):
        for e, i in ((0, S - 1), (2, 0)):
            where = pl.ds(place(0, t) + i, NP, stride=step)
            a, b = first[where, :], second[where, :]
            base = (t * 4 + e) * S
            lines[pl.ds(base, NP, stride=2), :] = jnp.where(low16, a, swap(b))
            lines[pl.ds(base + 1, NP, stride=2), :] = jnp.where(low16, swap(a), b)
        for e, pair in ((1, 0), (3, NP - 1)):
            where = pl.ds(place(pair, t), S)
            a, b = first[where, :], second[where, :]
            line = jnp.where(low32, a, swap(b)) if e == 1 else jnp.where(low32, swap(a), b)
            lines[pl.ds((t * 4 + e) * S, S), :] = line
        for corner, (e, s) in enumerate(((2, 0), (2, S - 1), (0, 0), (0, S - 1))):
            lines[pl.ds(LINES + t * 4 + corner, 1), :] = lines[pl.ds((t * 4 + e) * S + s, 1), :]
    lines[pl.ds(LINES + EDGES, HALF - EDGES), :] = jnp.zeros((HALF - EDGES, 128), F32)
    for j in range(EDGES):
        for h in range(2):
            out[h * EDGES + j] = lines[pl.ds(j * S + h * HALF, HALF), :].astype(BF)
    out[2 * EDGES] = lines[pl.ds(LINES, HALF), :].astype(BF)


def fill_pad(pad, src):
    for p in (0, PAIRS - 1):
        pad[pl.ds(p * PR, PR), :] = jnp.zeros((PR, 128), F32)
    for p in range(NP):
        for t in range(TL):
            base = (p + 1) * PR + rows_at(t)
            pad[pl.ds(base - 8, 8), :] = jnp.zeros((8, 128), F32)
            pad[pl.ds(base, S), :] = src[t * S : (t + 1) * S, p * 128 : (p + 1) * 128].astype(F32)
        pad[pl.ds((p + 1) * PR + 120, 8), :] = jnp.zeros((8, 128), F32)


def pad_place(pair, t):
    return (pair + 1) * PR + rows_at(t)


def flat_place(pair, t):
    return pair * R + t * S


def make_shifts(xp, pad):
    for a in range(3):
        for p in range(PAIRS):
            for t in range(TL):
                xp[a, p, t * S : (t + 1) * S, :] = pad[pl.ds(p * PR + rows_at(t) - 1 + a, S), :].astype(BF)


def build_forward(w_out, w):
    w_out[...] = jnp.zeros_like(w_out)
    for a in range(3):
        for c in range(3):
            block = w[a, c].astype(BF)
            for n in range(4):
                m = n + 1 + c
                w_out[a, m * C : (m + 1) * C, n * C : (n + 1) * C] = block


def build_backward(w_out, w_rim, w_corner, w):
    w_out[...] = jnp.zeros_like(w_out)
    w_rim[...] = jnp.zeros_like(w_rim)
    w_corner[...] = jnp.zeros_like(w_corner)
    for a in range(3):
        for c in range(3):
            block = w[a, c].T.astype(BF)
            for n in range(4):
                m = n + 3 - c
                w_out[2 - a, m * C : (m + 1) * C, n * C : (n + 1) * C] = block
            spots = []
            if a == 2:
                spots.append((0, c))
            if c == 0:
                spots.append((1, a))
            if a == 0:
                spots.append((2, c))
            if c == 2:
                spots.append((3, a))
            for e, tap in spots:
                w_rim[tap * 128 + C : tap * 128 + 128, e * C : (e + 1) * C] = block
            if a != 1 and c != 1:
                corner = (a // 2) * 2 + c // 2
                w_corner[C:128, corner * C : (corner + 1) * C] = block


def conv(xp, w):
    total = None
    for a in range(3):
        left = jnp.concatenate(
            [
                jnp.concatenate([xp[a, 2 * q + s] for q in range(NP // 2)], axis=0)
                for s in range(4)
            ],
            axis=1,
        )
        part = jnp.dot(left, w[a], preferred_element_type=F32)
        total = part if total is None else total + part
    return total


def columns(xp, a):
    return jnp.concatenate(
        [jnp.concatenate([xp[a, d + p] for p in range(NP)], axis=0) for d in range(3)], axis=1
    )


def first_part(xp, q, a):
    out = lax.dot_general(q, columns(xp, a), (((0,), (0,)), ((), ())), preferred_element_type=F32)
    turned = jnp.concatenate([out[:, d * 128 : (d + 1) * 128].T for d in range(3)], axis=0)
    return turned[64:256] + swap(turned[128:320])


def second_part(qp, h, a):
    out = lax.dot_general(h, columns(qp, 2 - a), (((0,), (0,)), ((), ())), preferred_element_type=F32)
    even, odd = out[:C], out[C:]
    return jnp.concatenate(
        [
            even[:, 128:256] + swap(odd[:, 256:384]),
            swap(even[:, 128:256]) + odd[:, 128:256],
            even[:, :128] + swap(odd[:, 128:256]),
        ],
        axis=0,
    )


def second_rims(grad, lines, wide, corners_ref, corner_row, codes, me):
    upper = jnp.logical_not(low_lanes(C))
    kept = [lines[pl.ds(j * S, S), :].astype(BF) for j in range(EDGES)]
    ours = [line.astype(BF) for line in reverse(kept, codes)]
    zero = jnp.zeros((S, 128), BF)
    left = jnp.concatenate(
        [
            jnp.concatenate([jnp.where(codes[j] % 4 == e, ours[j], zero) for j in range(EDGES)], axis=0)
            for e in range(4)
        ],
        axis=1,
    )
    out = lax.dot_general(left, wide[...], (((0,), (0,)), ((), ())), preferred_element_type=F32)
    pixels = lines[pl.ds(LINES, 16), :].astype(BF)
    pick = picked(corner_row, me)
    kind = lax.broadcasted_iota(jnp.int32, (16, 1024), 1) % 4
    for e in range(4):
        for c in range(3):
            a, b = ((2, c), (c, 0), (0, c), (c, 2))[e]
            at = pl.ds((a * 3 + b) * C, C)
            part = out[e * 128 : e * 128 + C, c * 128 : (c + 1) * 128]
            grad[at, :] = grad[at, :] + jnp.where(upper, part, 0.0)
        chosen = jnp.where(pick & (kind == e), 1.0, 0.0).astype(BF)
        met = jnp.dot(chosen, corners_ref[...], preferred_element_type=F32).astype(BF)
        part = lax.dot_general(pixels, met, (((0,), (0,)), ((), ())), preferred_element_type=F32)
        at = pl.ds(((e // 2) * 6 + (e % 2) * 2) * C, C)
        grad[at, :] = grad[at, :] + jnp.where(upper, part[:C], 0.0)


def reverse(kept, codes):
    flip = (
        lax.broadcasted_iota(jnp.int32, (S, S), 0) + lax.broadcasted_iota(jnp.int32, (S, S), 1)
        == S - 1
    )
    flip = jnp.where(flip, 1.0, 0.0).astype(BF)
    flipped = jnp.dot(flip, jnp.concatenate(kept, axis=1), preferred_element_type=F32)
    return [
        jnp.where(codes[j] >= 4, flipped[:, j * 128 : (j + 1) * 128], kept[j].astype(F32))
        for j in range(EDGES)
    ]


def orient(lines_ref, codes, w_rim, turned, wide):
    lines = lines_ref[...].astype(F32)
    low = low_lanes(S)
    spot = lax.broadcasted_iota(jnp.int32, (LINES, 128), 0) % S
    after = jnp.where(spot == S - 1, 0.0, pltpu.roll(lines, LINES - 1, 0)).astype(BF)
    before = jnp.where(spot == 0, 0.0, pltpu.roll(lines, 1, 0)).astype(BF)
    wide[...] = jnp.concatenate([after, lines_ref[...], before], axis=1)
    rims = jnp.dot(wide[...], w_rim[...], preferred_element_type=F32)
    kept = []
    for j in range(EDGES):
        e = codes[j] % 4
        at = slice(j * S, (j + 1) * S)
        pair = jnp.where(e >= 2, rims[at, 128:], rims[at, :128])
        rim = jnp.where(e % 2 == 1, pair, swap(pair))
        kept.append(jnp.where(low, lines[at], rim).astype(BF))
    for j, line in enumerate(reverse(kept, codes)):
        turned[pl.ds(j * S, S), :] = line


def halo_in(pad, turned, cells):
    low16 = low_lanes(16)
    cells_swapped = swap(cells[...])
    for t in range(TL):
        for e, row in ((0, rows_at(t) + S), (2, rows_at(t) - 1)):
            base = (t * 4 + e) * S
            even = turned[pl.ds(base, NP, stride=2), :]
            odd = turned[pl.ds(base + 1, NP, stride=2), :]
            pad[pl.ds(PR + row, NP, stride=PR), :] = jnp.where(low16, even, swap(odd))
        pad[pl.ds(rows_at(t), S), :] = swap(turned[pl.ds((t * 4 + 1) * S, S), :])
        pad[pl.ds((PAIRS - 1) * PR + rows_at(t), S), :] = turned[pl.ds((t * 4 + 3) * S, S), :]
        for corner, (row, p) in enumerate(((-1, 0), (-1, 1), (S, 0), (S, 1))):
            at = t * 4 + corner
            value = (cells[...] if p else cells_swapped)[at : at + 1]
            pad[pl.ds(p * (PAIRS - 1) * PR + rows_at(t) + row, 1), :] = value


def picked(corner_row, me):
    slot = lax.broadcasted_iota(jnp.int32, (16, 1024), 0)
    return (corner_row[...] == me * EDGES + slot) & (slot < EDGES)


def corner_sums(corners_ref, corner_row, me, w_corner):
    every = jnp.dot(corners_ref[...], w_corner[...], preferred_element_type=F32)
    kind = lax.broadcasted_iota(jnp.int32, (1024, 128), 0) % 4
    pair = jnp.where(kind >= 2, every[:, 128:], every[:, :128])
    other = swap(pair)
    low = low_lanes(1024)
    both = jnp.where((kind % 2 == 1) == low, other, pair).astype(BF)
    pick = picked(corner_row, me)
    return jnp.dot(jnp.where(pick, 1.0, 0.0).astype(BF), both, preferred_element_type=F32)


def rims_in(back, turned, sums):
    low16, low32, low1 = low_lanes(16), low_lanes(S), low_lanes(16)
    for t in range(TL):
        for e, i in ((0, S - 1), (2, 0)):
            base = (t * 4 + e) * S
            even = turned[pl.ds(base, NP, stride=2), :]
            odd = turned[pl.ds(base + 1, NP, stride=2), :]
            at = pl.ds(t * S + i, NP, stride=R)
            back[at, :] = back[at, :] + jnp.where(low16, swap(even), odd)
        at = pl.ds(t * S, S)
        line = swap(turned[pl.ds((t * 4 + 1) * S, S), :])
        back[at, :] = back[at, :] + jnp.where(low32, line, 0.0)
        at = pl.ds((NP - 1) * R + t * S, S)
        back[at, :] = back[at, :] + jnp.where(low32, 0.0, turned[pl.ds((t * 4 + 3) * S, S), :])
    lows, highs = jnp.where(low1, sums, 0.0), jnp.where(low1, 0.0, sums)
    for t in range(TL):
        for corner, (i, p) in enumerate(((0, 0), (0, 1), (S - 1, 0), (S - 1, 1))):
            at = pl.ds(p * (NP - 1) * R + t * S + i, 1)
            s = t * 4 + corner
            back[at, :] = back[at, :] + (highs if p else lows)[s : s + 1]


def both_convs(
    x_ref, q_ref, wf_ref, wb_ref, lines_ref, corners_ref, corner_row, tab, places,
    pad, xp, qp, w_conv, w_rim, w_corner, turned, wide, cells_all, cells, main, back,
):
    me = lax.axis_index("tile")
    codes = [tab[me * EDGES + j] // 2**21 for j in range(EDGES)]
    build_backward(w_conv, w_rim, w_corner, wb_ref)
    fill_pad(pad, q_ref)
    make_shifts(qp, pad)
    out = conv(qp, w_conv)
    for q in range(NP // 2):
        for half in range(2):
            back[pl.ds((2 * q + half) * R, R), :] = out[q * R : (q + 1) * R, half * 128 : (half + 1) * 128]
    orient(lines_ref, codes, w_rim, turned, wide)
    sums = corner_sums(corners_ref, corner_row, me, w_corner)
    rims_in(back, turned, sums)
    cells_all[...] = corners_ref[...].astype(F32)
    for s in range(EDGES):
        v = places[me * EDGES + s]
        tile = v // 4
        device = tile // 3
        row = device * 16 + (tile - device * 3) * 4 + v % 4
        cells[pl.ds(s, 1), :] = cells_all[pl.ds(row, 1), :]
    cells[pl.ds(EDGES, 4), :] = jnp.zeros((4, 128), F32)
    fill_pad(pad, x_ref)
    halo_in(pad, turned, cells)
    make_shifts(xp, pad)
    build_forward(w_conv, wf_ref)
    main[...] = conv(xp, w_conv)


CONV_SCRATCH = [
    pltpu.VMEM((PAIRS * PR, 128), F32),
    pltpu.VMEM((3, PAIRS, R, 128), BF),
    pltpu.VMEM((3, PAIRS, R, 128), BF),
    pltpu.VMEM((3, 512, 256), BF),
    pltpu.VMEM((384, 256), BF),
    pltpu.VMEM((128, 256), BF),
    pltpu.VMEM((LINES, 128), F32),
    pltpu.VMEM((LINES, 384), BF),
    pltpu.VMEM((1024, 128), F32),
    pltpu.VMEM((16, 128), F32),
    pltpu.VMEM((NP // 2 * R, 256), F32),
    pltpu.VMEM((NP * R, 128), F32),
]


def start_kernel(f_ref, c_ref, out, pad_a, pad_b, lines):
    fill_pad(pad_a, f_ref)
    fill_pad(pad_b, c_ref)
    put_lines(lines, pad_a, pad_b, pad_place, out)


def middle_kernel(
    f_ref, c_ref, w1_ref, w2_ref, lines_ref, corners_ref, corner_row, tab, places,
    hidden, pre_grad, grad, out,
    pad, xp, qp, w_conv, w_rim, w_corner, turned, wide, cells_all, cells, main, back, hid, lines, grads, hids,
):
    both_convs(
        f_ref, c_ref, w1_ref, w2_ref, lines_ref, corners_ref, corner_row, tab, places,
        pad, xp, qp, w_conv, w_rim, w_corner, turned, wide, cells_all, cells, main, back,
    )
    for p in range(NP):
        pre = main[pl.ds((p // 2) * R, R), (p % 2) * 128 : (p % 2) * 128 + 128]
        at = pl.ds(p * R, R)
        s = 1.0 / (1.0 + jnp.exp(-pre))
        h = (pre * s).astype(BF)
        g = (back[at, :] * s * (1.0 + pre * (1.0 - s))).astype(BF)
        hidden[:, p * 128 : (p + 1) * 128] = h
        pre_grad[:, p * 128 : (p + 1) * 128] = g
        hid[at, :] = h.astype(F32)
        back[at, :] = g.astype(F32)
        grads[at, :] = g
        hids[at, :] = h
    put_lines(lines, hid, back, flat_place, out)
    low = low_lanes(192)
    for a in range(3):
        grad[pl.ds(a * 192, 192), :] = jnp.where(
            low, first_part(xp, grads[...], a), second_part(qp, hids[...], a)
        )
    me = lax.axis_index("tile")
    codes = [tab[me * EDGES + j] // 2**21 for j in range(EDGES)]
    second_rims(grad, lines, wide, corners_ref, corner_row, codes, me)


def last_kernel(
    h_ref, g_ref, f_ref, c_ref, w1_ref, w2_ref, lines_ref, corners_ref, corner_row, tab, places, grads_ref,
    output, field_grad, grad_one, grad_two,
    pad, xp, qp, w_conv, w_rim, w_corner, turned, wide, cells_all, cells, main, back,
):
    both_convs(
        h_ref, g_ref, w2_ref, w1_ref, lines_ref, corners_ref, corner_row, tab, places,
        pad, xp, qp, w_conv, w_rim, w_corner, turned, wide, cells_all, cells, main, back,
    )
    for p in range(NP):
        at, lanes = pl.ds(p * R, R), slice(p * 128, (p + 1) * 128)
        made = main[pl.ds((p // 2) * R, R), (p % 2) * 128 : (p % 2) * 128 + 128]
        output[:, lanes] = (f_ref[:, lanes].astype(F32) + made).astype(BF)
        field_grad[:, lanes] = (c_ref[:, lanes].astype(F32) + back[at, :]).astype(BF)
    scale = 1.0 / math.sqrt(2 * 192 * S * S)
    grad_one[...] = grads_ref[:, :C] * scale
    grad_two[...] = grads_ref[:, C:] * scale


def exchange_kernel(with_total, x_ref, tab, *refs):
    t = lax.axis_index("tile")
    b = lax.axis_index("batch")
    z, y, x, core = t // 16, (t // 4) % 4, (t // 2) % 2, t % 2

    def index(z, y, x, core):
        return z * 16 + y * 4 + x * 2 + core

    if with_total:
        grads, out_lines, out_corners, out_grads, *refs = refs
        summed, parts, by_y, by_z, *refs = refs
    else:
        out_lines, out_corners, *refs = refs
    held_a, held_b, chosen, got_a, got_b, crossing, crossed, cells, sent, come = refs
    held, got = (held_a, held_b), (got_a, got_b)

    along_z = [(index((z + k) % 4, y, x, core), b) for k in range(1, 4)]
    along_y = [(index(z, (y + k) % 4, x, core), b) for k in range(1, 4)]
    sibling = (index(z, y, x, 1 - core), b)
    across = (index(z, y, 1 - x, core), b)
    group = x * 4 + b * 2 + core
    near = []
    for k in range(1, 8):
        g = (group + k) % 8
        near.append((index(z, y, g // 4, g % 2), (g // 2) % 2))
    partners = along_z + along_y + (near if with_total else [sibling, across])
    barrier = pltpu.get_barrier_semaphore()
    for other in partners:
        pl.semaphore_signal(barrier, inc=1, device_id=other, device_id_type=MESH)
    pl.semaphore_wait(barrier, len(partners))

    copies = []

    def remote(src, dst, other):
        n = len(copies)
        copy = pltpu.make_async_remote_copy(
            src_ref=src, dst_ref=dst, send_sem=sent.at[n], recv_sem=come.at[n],
            device_id=other, device_id_type=MESH,
        )
        copy.start()
        copies.append(copy)
        return copy

    def piece(ref, g):
        return ref.at[pl.ds(pl.multiple_of(g * SHARE, 8), SHARE)]

    chains = ((z, y, along_z, along_y), (y, z, along_y, along_z))
    first, over = [], []
    for h, (p, _, others, _) in enumerate(chains):
        mine = x_ref.at[pl.ds(h * EDGES, EDGES)]
        place = held[h].at[pl.ds((p * 2 + core) * EDGES, EDGES)]
        first.append([remote(mine, place, other) for other in others])
        over.append([remote(mine, place, sibling)])
        held[h][pl.ds((p * 2 + core) * EDGES, EDGES)] = x_ref[pl.ds(h * EDGES, EDGES)]
    cell = ((core * 4 + y) * 4 + z) * 2
    cells[cell + x] = x_ref[2 * EDGES]
    cell_x = remote(x_ref.at[2 * EDGES], cells.at[cell + x], across)
    if with_total:
        scatter = [
            remote(piece(grads, (group + k) % 8), parts.at[group], near[k - 1]) for k in range(1, 8)
        ]
        parts[group] = grads[pl.ds(pl.multiple_of(group * SHARE, 8), SHARE), :]
    for k in range(3):
        for h, (p, _, _, _) in enumerate(chains):
            first[h][k].wait_recv()
            here = held[h].at[pl.ds((((p + 3 - k) % 4) * 2 + core) * EDGES, EDGES)]
            over[h].append(remote(here, here, sibling))
    cell_x.wait_recv()
    here = cells.at[pl.ds(cell, 2)]
    cell_z = [remote(here, here, other) for other in along_z]

    second = []
    for h, (p, q, _, others) in enumerate(chains):
        for copy in over[h]:
            copy.wait_recv()
        second.append([])
        for k in range(4):
            to = (q + k) % 4
            base = (index(z, to, 0, core) if h == 0 else index(to, y, 0, core)) * EDGES

            def take(j, _, h=h, k=k, base=base):
                for side in range(2):
                    line = held[h][(tab[base + side * 2 * EDGES + j] >> (8 * h)) & 255]
                    chosen[h, k, side * EDGES + j] = line
                return 0

            lax.fori_loop(0, EDGES, take, 0)
            place = got[h].at[pl.ds(q * 2 * EDGES, 2 * EDGES)]
            if k:
                second[h].append(remote(chosen.at[h, k], place, others[k - 1]))
            else:
                got[h][pl.ds(q * 2 * EDGES, 2 * EDGES)] = chosen[h, 0]
    if with_total:
        for copy in scatter:
            copy.wait_recv()
        total = parts[0]
        for g in range(1, 8):
            total = total + parts[g]
        by_y[y] = total
        add_y = [remote(by_y.at[y], by_y.at[y], other) for other in along_y]
    for copy in cell_z:
        copy.wait_recv()
    here = cells.at[pl.ds((core * 4 + y) * 8, 8)]
    cell_y = [remote(here, here, other) for other in along_y]

    if with_total:
        for copy in add_y:
            copy.wait_recv()
        by_z[z] = ((by_y[0] + by_y[1]) + by_y[2]) + by_y[3]
        add_z = [remote(by_z.at[z], by_z.at[z], other) for other in along_z]

    third = []
    base = index(z, y, 1 - x, core) * EDGES
    for h in range(2):
        for copy in second[h]:
            copy.wait_recv()

        def pass_on(j, _, h=h):
            crossing[h, j] = got[h][((tab[base + j] >> (16 + 2 * h)) & 3) * (2 * EDGES) + (1 - x) * EDGES + j]
            return 0

        lax.fori_loop(0, EDGES, pass_on, 0)
        third.append(remote(crossing.at[h], crossed.at[h], across))
    if with_total:
        for copy in add_z:
            copy.wait_recv()
        total = ((by_z[0] + by_z[1]) + by_z[2]) + by_z[3]
        summed[...] = total
        out_grads[pl.ds(pl.multiple_of(group * SHARE, 8), SHARE), :] = total
        gather = [remote(summed, piece(out_grads, group), other) for other in near]
    for copy in cell_y:
        copy.wait_recv()
    here = cells.at[pl.ds(core * 32, 32)]
    last = remote(here, here, sibling)

    for h in range(2):
        third[h].wait_recv()

        def give(j, _, h=h):
            entry = tab[t * EDGES + j]
            straight = got[h][((entry >> (16 + 2 * h)) & 3) * (2 * EDGES) + x * EDGES + j]
            near = ((entry >> 20) & 1) == x
            at = pl.ds(pl.multiple_of(j * S + h * HALF, HALF), HALF)
            out_lines[at, :] = jnp.where(near, straight, crossed[h, j])
            return 0

        lax.fori_loop(0, EDGES, give, 0)
    last.wait_recv()
    for d in range(64):
        out_corners[d * HALF : (d + 1) * HALF, :] = cells[
            (((d % 2) * 4 + (d // 4) % 4) * 4 + d // 16) * 2 + (d // 2) % 2
        ]
    if with_total:
        for copy in gather:
            copy.wait_recv()
    for copy in copies:
        copy.wait_send()


def exchange(lines, tab, ident, grads=None):
    n = 6 + 2 + 1 + 6 + 3 + 6 + 3 + 2 + 1
    outs = [jax.ShapeDtypeStruct((LINES, 128), BF), jax.ShapeDtypeStruct((1024, 128), BF)]
    scratch = []
    if grads is not None:
        n += 7 + 3 + 3 + 7
        outs.append(jax.ShapeDtypeStruct((8 * SHARE, 128), F32))
        scratch = [pltpu.VMEM((k, SHARE, 128), F32) for k in (8, 4, 4)]
        scratch = [pltpu.VMEM((SHARE, 128), F32)] + scratch
    return pl.pallas_call(
        functools.partial(exchange_kernel, grads is not None),
        out_shape=tuple(outs),
        in_specs=[VM, SM] + [VM] * len(outs[2:]),
        out_specs=(VM,) * len(outs),
        scratch_shapes=scratch
        + [
            pltpu.VMEM((8 * EDGES, HALF, 128), BF),
            pltpu.VMEM((8 * EDGES, HALF, 128), BF),
            pltpu.VMEM((2, 4, 2 * EDGES, HALF, 128), BF),
            pltpu.VMEM((8 * EDGES, HALF, 128), BF),
            pltpu.VMEM((8 * EDGES, HALF, 128), BF),
            pltpu.VMEM((2, EDGES, HALF, 128), BF),
            pltpu.VMEM((2, EDGES, HALF, 128), BF),
            pltpu.VMEM((64, HALF, 128), BF),
            pltpu.SemaphoreType.DMA((n,)),
            pltpu.SemaphoreType.DMA((n,)),
        ],
        name="exchange_and_total" if scratch else "exchange",
        compiler_params=pltpu.CompilerParams(
            collective_id=ident, has_side_effects=True, vmem_limit_bytes=40 * 2**20
        ),
    )(lines, tab, *([] if grads is None else [grads]))


def tables(adjacency, seam_codes):
    source, tile = adjacency // TL, adjacency % TL
    line = tile * 4 + seam_codes % 4
    z, y, x, core = source // 16, (source // 4) % 4, (source // 2) % 2, source % 2
    by_z, by_y = (z * 2 + core) * EDGES + line, (y * 2 + core) * EDGES + line
    return by_z + by_y * 2**8 + y * 2**16 + z * 2**18 + x * 2**20 + seam_codes * 2**21


def body(fields, cotangent, first_kernel, second_kernel, adjacency, seam_codes, corner_map):
    f = fields.reshape(R, S * C)
    c = cotangent.reshape(R, S * C)
    tab = tables(adjacency, seam_codes).reshape(768)
    places = corner_map.reshape(768)
    corner_row = jnp.pad(corner_map.reshape(64, EDGES), ((0, 0), (0, 4)), constant_values=-1)
    corner_row = corner_row.reshape(1, 1024)
    wide = jax.ShapeDtypeStruct((R, S * C), BF)
    sent = jax.ShapeDtypeStruct((2 * EDGES + 1, HALF, 128), BF)
    sums = jax.ShapeDtypeStruct((576, 128), F32)
    params = pltpu.CompilerParams(vmem_limit_bytes=48 * 2**20)

    lines = pl.pallas_call(
        start_kernel,
        out_shape=sent,
        in_specs=[VM, VM],
        out_specs=VM,
        scratch_shapes=[
            pltpu.VMEM((PAIRS * PR, 128), F32),
            pltpu.VMEM((PAIRS * PR, 128), F32),
            pltpu.VMEM((LINES + HALF, 128), F32),
        ],
        name="lines",
        compiler_params=params,
    )(f, c)
    near, cells = exchange(lines, tab, 0)
    hidden, pre_grad, grads, lines = pl.pallas_call(
        middle_kernel,
        out_shape=(wide, wide, sums, sent),
        in_specs=[VM] * 7 + [SM, SM],
        out_specs=(VM,) * 4,
        scratch_shapes=CONV_SCRATCH
        + [
            pltpu.VMEM((NP * R, 128), F32),
            pltpu.VMEM((LINES + HALF, 128), F32),
            pltpu.VMEM((NP * R, 128), BF),
            pltpu.VMEM((NP * R, 128), BF),
        ],
        name="middle",
        compiler_params=params,
    )(f, c, first_kernel, second_kernel, near, cells, corner_row, tab, places)
    near, cells, grads = exchange(lines, tab, 1, grads)
    kernel_sums = jax.ShapeDtypeStruct((9 * C, C), F32)
    output, field_grad, grad_one, grad_two = pl.pallas_call(
        last_kernel,
        out_shape=(wide, wide, kernel_sums, kernel_sums),
        in_specs=[VM] * 9 + [SM, SM, VM],
        out_specs=(VM,) * 4,
        scratch_shapes=CONV_SCRATCH,
        name="last",
        compiler_params=params,
    )(hidden, pre_grad, f, c, first_kernel, second_kernel, near, cells, corner_row, tab, places, grads)
    shape_out = (1, TL, S, S * C)
    return (
        output.reshape(shape_out),
        field_grad.reshape(shape_out),
        grad_one.reshape(3, 3, C, C),
        grad_two.reshape(3, 3, C, C),
    )


def solution(mesh):
    split = P("batch", "tile", None, None)
    return jax.shard_map(
        body,
        mesh=mesh,
        in_specs=(split, split, P(), P(), P(), P(), P()),
        out_specs=(split, split, P(), P()),
        check_vma=False,
    )
```

time: 99 us -> 71.3 us (0.72)
  Pallas kernels: 93.5 us -> 67.2 us
  other arithmetic: 1.95 us -> 0.8 us
    pallas_call x4 -> x3, Pallas kernels: 88.2 us -> 60.4 us  [the longest x2 55.2 us: exchange(): pl.pallas_call(functools.partial(exchange_kernel, grads is not None), out...]
    mul x1 -> x0, other arithmetic: 1.95 us -> none  [body(): grads[:, C:].reshape(3, 3, C, C) * grad_scale]
    pallas_call x1, Pallas kernels: 5.06 us -> 6.54 us  [body(): pl.pallas_call(middle_kernel, out_shape=(wide, wide, sums, sent), in_spec...]
    unnamed x21 -> x9, local copies, waits for them, and re-layouts: 2.03 us -> 1.8 us
where the time goes in v2:
time: 71.3 us; the launch traced here: 71.1 us
  Pallas kernels  67.2 us (94%)
  local copies, waits for them, and re-layouts  2.31 us (3%)
  other arithmetic  0.8 us (1%)
  between operations  0.73 us (1%)
    pallas_call x2, Pallas kernels, exchange(): pl.pallas_call(functools.partial(exchange_kernel, grads is not None), out...  55.2 us
    pallas_call x1, Pallas kernels, body(): pl.pallas_call(middle_kernel, out_shape=(wide, wide, sums, sent), in_spec...  6.54 us
    pallas_call x1, Pallas kernels, body(): pl.pallas_call(last_kernel, out_shape=(wide, wide, kernel_sums, kernel_su...  5.22 us
    unnamed x9, local copies, waits for them, and re-layouts  1.8 us

profile of v2, /device:TPU:1, one launch (start us, length us, event | category | flops | bytes accessed | tf_op | source)
XLA Modules:
  0.0 71.1 jit_solution(993312016380167802)
XLA Ops:
  0.6 0.0 copy-start
  0.6 0.8 %fusion.9 = s32[192,4]{0,1:T(4,128)S(1)} fusion(s32[192,4]{0,1:T(4,128)} %param.12, s32[192,4]{0,1:T(4,128)} %param.11), kind=kLoop, calls=%fused_computation.31 | loop fusion | flops 79872 | bytes 9216 | tf_op jit(solution)/shard_map/add | solution.py:585
  1.4 0.1 copy.11
  1.6 0.1 reshape.40.tab
  1.7 0.8 %copy.12 = s32[192,4]{1,0:T(8,128)S(1)} copy(s32[192,4]{0,1:T(4,128)} %param.13) | data formatting | bytes 6144 | tf_op args[6]
  2.5 0.1 reshape.43.places
  2.6 0.1 reshape.41
  2.7 0.1 reshape.42.corner_row
  2.8 0.0 copy-done
  2.8 0.0 copy-start.1
  2.8 1.0 %copy-done.1 = bf16[1,3,32,2048]{3,2,1,0:T(8,128)(2,1)S(1)} copy-done((bf16[1,3,32,2048]{3,2,1,0:T(8,128)(2,1)S(1)}, bf16[1,3,32,2048]{3,2,1,0:T(8,128)(2,1)}, u32[]{:S(2)}) %copy-start.1) | copy-done | bytes 393240
  3.8 0.0 copy-start.2
  3.8 0.0 copy-start.3
  3.8 0.2 lines.1.x_ref
  4.0 25.7 %exchange.1 = (bf16[384,128]{1,0:T(8,128)(2,1)S(1)}, bf16[1024,128]{1,0:T(8,128)(2,1)S(1)}) custom-call(bf16[25,16,128]{2,1,0:T(8,128)(2,1)S(1)} %lines.1.x_ref, s32[768]{0:T(1024)S(1)} %reshape.40.tab), custom_call_target="tpu_custom_call" | custom-call | tf_op jit(solution)/shard_map/exchange/pallas_call | solution.py:555
  29.8 0.0 copy-done.2
  29.8 0.0 copy-done.3
  29.8 6.5 %middle.1 = (bf16[96,2048]{1,0:T(8,128)(2,1)S(1)}, bf16[96,2048]{1,0:T(8,128)(2,1)S(1)}, f32[576,128]{1,0:T(8,128)S(1)}, bf16[25,16,128]{2,1,0:T(8,128)(2,1)S(1)}) custom-call(bf16[96,2048]{1,0:T(8,128)(2,1)S(1)} %bitcast.7, bf16[96,2048]{1,0:T(8,128)(2,1)S(1)} %bitcast.10, f32[3,3,64,64]{3,2,1,0:T(8,128)S(1)} %copy-done.2, f32[3,3,64,64]{3,2,1,0:T(8,128)S(1)} %copy-done.3, ...), custom_call_target="tpu_custom_call" | custom-call | tf_op jit(solution)/shard_map/middle/pallas_call | solution.py:614
  36.4 29.5 %exchange_and_total.1 = (bf16[384,128]{1,0:T(8,128)(2,1)S(1)}, bf16[1024,128]{1,0:T(8,128)(2,1)S(1)}, f32[576,128]{1,0:T(8,128)S(1)}) custom-call(bf16[25,16,128]{2,1,0:T(8,128)(2,1)S(1)} %get-tuple-element.21.x_ref, s32[768]{0:T(1024)S(1)} %reshape.40.tab, f32[576,128]{1,0:T(8,128)S(1)} %get-tuple-element.22.refs_0_), custom_call_target="tpu_custom_call" | custom-call | tf_op jit(solution)/shard_map/exchange_and_total/pallas_call | solution.py:555
  65.8 5.2 %last.1 = (bf16[96,2048]{1,0:T(8,128)(2,1)}, bf16[96,2048]{1,0:T(8,128)(2,1)}, f32[576,64]{1,0:T(8,128)}, f32[576,64]{1,0:T(8,128)}) custom-call(bf16[96,2048]{1,0:T(8,128)(2,1)S(1)} %get-tuple-element.19.h_ref, bf16[96,2048]{1,0:T(8,128)(2,1)S(1)} %get-tuple-element.20.g_ref, bf16[96,2048]{1,0:T(8,128)(2,1)S(1)} %bitcast.8, bf16[96,2048]{1,0:T(8,128)(2,1)S(1)} %bitcast.11, ...), custom_call_target="tpu_custom_call" | custom-call | tf_op jit(solution)/shard_map/last/pallas_call | solution.py:631
  (1 shorter events, 0.0 us)
Async XLA Ops:
  0.6 2.2 %copy-start = (bf16[1,3,32,2048]{3,2,1,0:T(8,128)(2,1)S(1)}, bf16[1,3,32,2048]{3,2,1,0:T(8,128)(2,1)}, u32[]{:S(2)}) copy-start(bf16[1,3,32,2048]{3,2,1,0:T(8,128)(2,1)} %param.7) | copy-start | bytes 1179652
  2.8 1.0 %copy-start.1 = (bf16[1,3,32,2048]{3,2,1,0:T(8,128)(2,1)S(1)}, bf16[1,3,32,2048]{3,2,1,0:T(8,128)(2,1)}, u32[]{:S(2)}) copy-start(bf16[1,3,32,2048]{3,2,1,0:T(8,128)(2,1)} %param.8) | copy-start | bytes 1179652
  3.8 26.0 %copy-start.2 = (f32[3,3,64,64]{3,2,1,0:T(8,128)S(1)}, f32[3,3,64,64]{3,2,1,0:T(8,128)}, u32[]{:S(2)}) copy-start(f32[3,3,64,64]{3,2,1,0:T(8,128)} %w1_ref.3) | copy-start | bytes 442372
  3.8 26.0 %copy-start.3 = (f32[3,3,64,64]{3,2,1,0:T(8,128)S(1)}, f32[3,3,64,64]{3,2,1,0:T(8,128)}, u32[]{:S(2)}) copy-start(f32[3,3,64,64]{3,2,1,0:T(8,128)} %w2_ref.3) | copy-start | bytes 442372

commit v3 on v2

v3 whole, which is shorter than its diff:
```python
import math

import jax
import jax.numpy as jnp
from jax import lax
from jax.experimental import pallas as pl
from jax.experimental.pallas import tpu as pltpu
from jax.sharding import PartitionSpec as P

TL = 3
S = 32
C = 64
NP = 16
R = TL * S
EDGES = TL * 4
LINES = EDGES * S
HALF = S // 2
SHARE = 9 * C // 8
PAIRS = NP + 2
PR = 128
MESH = pl.DeviceIdType.MESH
F32 = jnp.float32
BF = jnp.bfloat16
VM = pl.BlockSpec(memory_space=pltpu.VMEM)


def rows_at(t):
    return t * 40 + 8


def low_lanes(rows):
    return lax.broadcasted_iota(jnp.int32, (rows, 128), 1) < C


def swap(v):
    return pltpu.roll(v, C, 1)


def put_lines(lines, first, second, place, out):
    low16, low32 = low_lanes(16), low_lanes(32)
    step = place(1, 0) - place(0, 0)
    for t in range(TL):
        for e, i in ((0, S - 1), (2, 0)):
            where = pl.ds(place(0, t) + i, NP, stride=step)
            a, b = first[where, :], second[where, :]
            base = (t * 4 + e) * S
            lines[pl.ds(base, NP, stride=2), :] = jnp.where(low16, a, swap(b))
            lines[pl.ds(base + 1, NP, stride=2), :] = jnp.where(low16, swap(a), b)
        for e, pair in ((1, 0), (3, NP - 1)):
            where = pl.ds(place(pair, t), S)
            a, b = first[where, :], second[where, :]
            line = jnp.where(low32, a, swap(b)) if e == 1 else jnp.where(low32, swap(a), b)
            lines[pl.ds((t * 4 + e) * S, S), :] = line
        for corner, (e, s) in enumerate(((2, 0), (2, S - 1), (0, 0), (0, S - 1))):
            lines[pl.ds(LINES + t * 4 + corner, 1), :] = lines[pl.ds((t * 4 + e) * S + s, 1), :]
    lines[pl.ds(LINES + EDGES, HALF - EDGES), :] = jnp.zeros((HALF - EDGES, 128), F32)
    for j in range(EDGES):
        for h in range(2):
            out[h * EDGES + j] = lines[pl.ds(j * S + h * HALF, HALF), :].astype(BF)
    out[2 * EDGES] = lines[pl.ds(LINES, HALF), :].astype(BF)


def fill_pad(pad, src):
    for p in (0, PAIRS - 1):
        pad[pl.ds(p * PR, PR), :] = jnp.zeros((PR, 128), F32)
    for p in range(NP):
        for t in range(TL):
            base = (p + 1) * PR + rows_at(t)
            pad[pl.ds(base - 8, 8), :] = jnp.zeros((8, 128), F32)
            pad[pl.ds(base, S), :] = src[t * S : (t + 1) * S, p * 128 : (p + 1) * 128].astype(F32)
        pad[pl.ds((p + 1) * PR + 120, 8), :] = jnp.zeros((8, 128), F32)


def pad_place(pair, t):
    return (pair + 1) * PR + rows_at(t)


def flat_place(pair, t):
    return pair * R + t * S


def make_shifts(xp, pad):
    for a in range(3):
        for p in range(PAIRS):
            for t in range(TL):
                xp[a, p, t * S : (t + 1) * S, :] = pad[pl.ds(p * PR + rows_at(t) - 1 + a, S), :].astype(BF)


def build_forward(w_out, w):
    w_out[...] = jnp.zeros_like(w_out)
    for a in range(3):
        for c in range(3):
            block = w[a, c].astype(BF)
            for n in range(4):
                m = n + 1 + c
                w_out[a, m * C : (m + 1) * C, n * C : (n + 1) * C] = block


def build_backward(w_out, w_rim, w_corner, w):
    w_out[...] = jnp.zeros_like(w_out)
    w_rim[...] = jnp.zeros_like(w_rim)
    w_corner[...] = jnp.zeros_like(w_corner)
    for a in range(3):
        for c in range(3):
            block = w[a, c].T.astype(BF)
            for n in range(4):
                m = n + 3 - c
                w_out[2 - a, m * C : (m + 1) * C, n * C : (n + 1) * C] = block
            spots = []
            if a == 2:
                spots.append((0, c))
            if c == 0:
                spots.append((1, a))
            if a == 0:
                spots.append((2, c))
            if c == 2:
                spots.append((3, a))
            for e, tap in spots:
                w_rim[tap * 128 + C : tap * 128 + 128, e * C : (e + 1) * C] = block
            if a != 1 and c != 1:
                corner = (a // 2) * 2 + c // 2
                for half in range(2):
                    w_corner[C:128, corner * 128 + half * C : corner * 128 + (half + 1) * C] = block


def conv(xp, w):
    total = None
    for a in range(3):
        left = jnp.concatenate(
            [
                jnp.concatenate([xp[a, 2 * q + s] for q in range(NP // 2)], axis=0)
                for s in range(4)
            ],
            axis=1,
        )
        part = jnp.dot(left, w[a], preferred_element_type=F32)
        total = part if total is None else total + part
    return total


def columns(xp, a):
    return jnp.concatenate(
        [jnp.concatenate([xp[a, d + p] for p in range(NP)], axis=0) for d in range(3)], axis=1
    )


def first_part(xp, q, a):
    out = lax.dot_general(q, columns(xp, a), (((0,), (0,)), ((), ())), preferred_element_type=F32)
    turned = jnp.concatenate([out[:, d * 128 : (d + 1) * 128].T for d in range(3)], axis=0)
    return turned[64:256] + swap(turned[128:320])


def second_part(qp, h, a):
    out = lax.dot_general(h, columns(qp, 2 - a), (((0,), (0,)), ((), ())), preferred_element_type=F32)
    even, odd = out[:C], out[C:]
    return jnp.concatenate(
        [
            even[:, 128:256] + swap(odd[:, 256:384]),
            swap(even[:, 128:256]) + odd[:, 128:256],
            even[:, :128] + swap(odd[:, 128:256]),
        ],
        axis=0,
    )


def second_rims(grad, lines, wide, corners_ref, corner_rows, codes, me):
    upper = jnp.logical_not(low_lanes(C))
    kept = [lines[pl.ds(j * S, S), :].astype(BF) for j in range(EDGES)]
    ours = [line.astype(BF) for line in reverse(kept, codes)]
    zero = jnp.zeros((S, 128), BF)
    left = jnp.concatenate(
        [
            jnp.concatenate([jnp.where(codes[j] % 4 == e, ours[j], zero) for j in range(EDGES)], axis=0)
            for e in range(4)
        ],
        axis=1,
    )
    out = lax.dot_general(left, wide[...], (((0,), (0,)), ((), ())), preferred_element_type=F32)
    pixels = lines[pl.ds(LINES, 16), :].astype(BF)
    for e in range(4):
        for c in range(3):
            a, b = ((2, c), (c, 0), (0, c), (c, 2))[e]
            at = pl.ds((a * 3 + b) * C, C)
            part = out[e * 128 : e * 128 + C, c * 128 : (c + 1) * 128]
            grad[at, :] = grad[at, :] + jnp.where(upper, part, 0.0)
        met = jnp.dot(
            picked(corner_rows, me, e), corners_ref[pl.ds(e * 256, 256), :], preferred_element_type=F32
        ).astype(BF)
        part = lax.dot_general(pixels, met, (((0,), (0,)), ((), ())), preferred_element_type=F32)
        at = pl.ds(((e // 2) * 6 + (e % 2) * 2) * C, C)
        grad[at, :] = grad[at, :] + jnp.where(upper, part[:C], 0.0)


def reverse(kept, codes):
    flip = (
        lax.broadcasted_iota(jnp.int32, (S, S), 0) + lax.broadcasted_iota(jnp.int32, (S, S), 1)
        == S - 1
    )
    flip = jnp.where(flip, 1.0, 0.0).astype(BF)
    flipped = jnp.dot(flip, jnp.concatenate(kept, axis=1), preferred_element_type=F32)
    return [
        jnp.where(codes[j] >= 4, flipped[:, j * 128 : (j + 1) * 128], kept[j].astype(F32))
        for j in range(EDGES)
    ]


def orient(lines_ref, codes, w_rim, turned, wide):
    lines = lines_ref[...].astype(F32)
    low = low_lanes(S)
    spot = lax.broadcasted_iota(jnp.int32, (LINES, 128), 0) % S
    after = jnp.where(spot == S - 1, 0.0, pltpu.roll(lines, LINES - 1, 0)).astype(BF)
    before = jnp.where(spot == 0, 0.0, pltpu.roll(lines, 1, 0)).astype(BF)
    wide[...] = jnp.concatenate([after, lines_ref[...], before], axis=1)
    rims = jnp.dot(wide[...], w_rim[...], preferred_element_type=F32)
    kept = []
    for j in range(EDGES):
        e = codes[j] % 4
        at = slice(j * S, (j + 1) * S)
        pair = jnp.where(e >= 2, rims[at, 128:], rims[at, :128])
        rim = jnp.where(e % 2 == 1, pair, swap(pair))
        kept.append(jnp.where(low, lines[at], rim).astype(BF))
    for j, line in enumerate(reverse(kept, codes)):
        turned[pl.ds(j * S, S), :] = line


def halo_in(pad, turned, cells):
    low16 = low_lanes(16)
    cells_swapped = swap(cells[...])
    for t in range(TL):
        for e, row in ((0, rows_at(t) + S), (2, rows_at(t) - 1)):
            base = (t * 4 + e) * S
            even = turned[pl.ds(base, NP, stride=2), :]
            odd = turned[pl.ds(base + 1, NP, stride=2), :]
            pad[pl.ds(PR + row, NP, stride=PR), :] = jnp.where(low16, even, swap(odd))
        pad[pl.ds(rows_at(t), S), :] = swap(turned[pl.ds((t * 4 + 1) * S, S), :])
        pad[pl.ds((PAIRS - 1) * PR + rows_at(t), S), :] = turned[pl.ds((t * 4 + 3) * S, S), :]
        for corner, (row, p) in enumerate(((-1, 0), (-1, 1), (S, 0), (S, 1))):
            at = t * 4 + corner
            value = (cells[...] if p else cells_swapped)[at : at + 1]
            pad[pl.ds(p * (PAIRS - 1) * PR + rows_at(t) + row, 1), :] = value


def picked(corner_rows, me, kind):
    slot = lax.broadcasted_iota(jnp.int32, (16, 256), 0)
    pick = (corner_rows[kind : kind + 1, :] == me * EDGES + slot) & (slot < EDGES)
    return jnp.where(pick, 1.0, 0.0).astype(BF)


def corner_sums(corners_ref, corner_rows, me, w_corner):
    total = None
    for kind in range(4):
        rim = jnp.dot(
            corners_ref[pl.ds(kind * 256, 256), :],
            w_corner[:, kind * 128 : (kind + 1) * 128],
            preferred_element_type=F32,
        ).astype(BF)
        part = jnp.dot(picked(corner_rows, me, kind), rim, preferred_element_type=F32)
        total = part if total is None else total + part
    return total


def rims_in(back, turned, sums):
    low16, low32, low1 = low_lanes(16), low_lanes(S), low_lanes(16)
    for t in range(TL):
        for e, i in ((0, S - 1), (2, 0)):
            base = (t * 4 + e) * S
            even = turned[pl.ds(base, NP, stride=2), :]
            odd = turned[pl.ds(base + 1, NP, stride=2), :]
            at = pl.ds(t * S + i, NP, stride=R)
            back[at, :] = back[at, :] + jnp.where(low16, swap(even), odd)
        at = pl.ds(t * S, S)
        line = swap(turned[pl.ds((t * 4 + 1) * S, S), :])
        back[at, :] = back[at, :] + jnp.where(low32, line, 0.0)
        at = pl.ds((NP - 1) * R + t * S, S)
        back[at, :] = back[at, :] + jnp.where(low32, 0.0, turned[pl.ds((t * 4 + 3) * S, S), :])
    lows, highs = jnp.where(low1, sums, 0.0), jnp.where(low1, 0.0, sums)
    for t in range(TL):
        for corner, (i, p) in enumerate(((0, 0), (0, 1), (S - 1, 0), (S - 1, 1))):
            at = pl.ds(p * (NP - 1) * R + t * S + i, 1)
            s = t * 4 + corner
            back[at, :] = back[at, :] + (highs if p else lows)[s : s + 1]


def cells_of(corners_ref, places, me):
    slot = lax.broadcasted_iota(jnp.int32, (16, 1024), 0)
    row = jnp.full((16, 1024), -1, jnp.int32)
    for s in range(EDGES):
        v = places[s % 4, me * TL + s // 4]
        row = jnp.where(slot == s, (v & 3) * 256 + (v >> 2), row)
    pick = jnp.where(lax.broadcasted_iota(jnp.int32, (16, 1024), 1) == row, 1.0, 0.0).astype(BF)
    return jnp.dot(pick, corners_ref[...], preferred_element_type=F32)


def codes_of(seams, me):
    return [seams[j % 4, me * TL + j // 4] for j in range(EDGES)]


def load_rows(corner_rows, rows):
    corner_rows[...] = jnp.full((8, 256), -1, jnp.int32)
    corner_rows[0:4, 0:192] = rows[...]


def put_back(back, out):
    for q in range(NP // 2):
        for half in range(2):
            back[pl.ds((2 * q + half) * R, R), :] = out[q * R : (q + 1) * R, half * 128 : (half + 1) * 128]


def first_kernel_body(
    f_hbm, c_hbm, w1_hbm, w2_hbm, adjacency_hbm, seams_hbm, places_hbm,
    hidden_hbm, back_hbm, w_rim_two, w_corner_two, near_two, corners_two, out_grads,
    f_ref, c_ref, w1_ref, w2_ref, adjacency, seams, places, rows, loads, stores, corner_rows,
    hidden, back_two, index,
    pad_f, pad_c, xp, qp, w_back, w_forth, w_rim, w_corner, turned, wide, cells, main, back,
    hid, lines, grads, hids, grad, sent_one, sent_two, near, corners, *refs,
):
    me = lax.axis_index("tile")
    inputs = [
        pltpu.make_async_copy(src, dst, loads.at[n])
        for n, (src, dst) in enumerate(
            (
                (f_hbm, f_ref), (c_hbm, c_ref), (w2_hbm, w2_ref), (w1_hbm, w1_ref),
                (adjacency_hbm, adjacency), (seams_hbm, seams), (places_hbm, places), (places_hbm, rows),
            )
        )
    ]
    for copy in inputs:
        copy.start()
    mesh = Mesh()
    mesh.greet()
    n = len(ROUND)
    one, two, rest = refs[:n], refs[n : 2 * n], refs[2 * n :]
    summed, parts, by_y, by_z, sent, come = rest
    net = Net(sent, come)
    inputs[0].wait()
    fill_pad(pad_f, f_ref)
    inputs[1].wait()
    fill_pad(pad_c, c_ref)
    put_lines(lines, pad_f, pad_c, pad_place, sent_one)
    mesh.meet()
    first = exchange_steps(mesh, net, index, sent_one, near, corners, one)
    next(first)
    for copy in inputs[4:]:
        copy.wait()
    find_index(mesh, adjacency, seams, index)
    load_rows(corner_rows, rows)
    make_shifts(qp, pad_c)
    inputs[2].wait()
    build_backward(w_back, w_rim, w_corner, w2_ref)
    next(first)
    put_back(back, conv(qp, w_back))
    next(first)
    inputs[3].wait()
    build_forward(w_forth, w1_ref)
    next(first)
    next(first)

    codes = codes_of(seams, me)
    orient(near, codes, w_rim, turned, wide)
    cells[...] = cells_of(corners, places, me)
    halo_in(pad_f, turned, cells)
    make_shifts(xp, pad_f)
    rims_in(back, turned, corner_sums(corners, corner_rows, me, w_corner))
    main[...] = conv(xp, w_forth)
    for p in range(NP):
        pre = main[pl.ds((p // 2) * R, R), (p % 2) * 128 : (p % 2) * 128 + 128]
        at = pl.ds(p * R, R)
        s = 1.0 / (1.0 + jnp.exp(-pre))
        h = (pre * s).astype(BF)
        g = (back[at, :] * s * (1.0 + pre * (1.0 - s))).astype(BF)
        hidden[:, p * 128 : (p + 1) * 128] = h
        hid[at, :] = h.astype(F32)
        back[at, :] = g.astype(F32)
        grads[at, :] = g
        hids[at, :] = h
    put_lines(lines, hid, back, flat_place, sent_two)
    second = exchange_steps(mesh, net, index, sent_two, near_two, corners_two, two)
    next(second)
    outputs = [
        pltpu.make_async_copy(hidden, hidden_hbm, stores.at[0]),
        pltpu.make_async_copy(back_two, back_hbm, stores.at[1]),
    ]
    outputs[0].start()

    low = low_lanes(192)
    for a in range(3):
        grad[pl.ds(a * 192, 192), :] = jnp.where(
            low, first_part(xp, grads[...], a), second_part(qp, hids[...], a)
        )
    second_rims(grad, lines, wide, corners, corner_rows, codes, me)
    adding = total_steps(mesh, net, grad, out_grads, summed, parts, by_y, by_z)
    next(adding)
    next(second)
    for p in range(NP):
        for t in range(TL):
            pad_c[pl.ds(pad_place(p, t), S), :] = back[pl.ds(flat_place(p, t), S), :]
    build_backward(w_back, w_rim_two, w_corner_two, w1_ref)
    next(second)
    make_shifts(qp, pad_c)
    next(adding)
    put_back(back_two, conv(qp, w_back))
    outputs[1].start()
    next(second)
    next(adding)
    next(adding)
    next(second)
    next(adding)
    net.finish()
    for copy in outputs:
        copy.wait()


def last_kernel_body(
    h_hbm, back_hbm, f_ref, c_ref, w2_ref, w_rim, w_corner, near, corners, seams_hbm, places_hbm, grads,
    output, field_grad, grad_one, grad_two,
    h_ref, back, seams, places, rows, loads, corner_rows, pad, xp, w_forth, turned, wide, cells, main,
):
    me = lax.axis_index("tile")
    inputs = [
        pltpu.make_async_copy(src, dst, loads.at[n])
        for n, (src, dst) in enumerate(
            (
                (seams_hbm, seams), (places_hbm, places), (places_hbm, rows), (h_hbm, h_ref),
                (back_hbm, back),
            )
        )
    ]
    for copy in inputs:
        copy.start()
    build_forward(w_forth, w2_ref)
    for copy in inputs:
        copy.wait()
    load_rows(corner_rows, rows)
    orient(near, codes_of(seams, me), w_rim, turned, wide)
    cells[...] = cells_of(corners, places, me)
    fill_pad(pad, h_ref)
    halo_in(pad, turned, cells)
    make_shifts(xp, pad)
    main[...] = conv(xp, w_forth)
    rims_in(back, turned, corner_sums(corners, corner_rows, me, w_corner))
    for p in range(NP):
        at, lanes = pl.ds(p * R, R), slice(p * 128, (p + 1) * 128)
        made = main[pl.ds((p // 2) * R, R), (p % 2) * 128 : (p % 2) * 128 + 128]
        output[:, lanes] = (f_ref[:, lanes].astype(F32) + made).astype(BF)
        field_grad[:, lanes] = (c_ref[:, lanes].astype(F32) + back[at, :]).astype(BF)
    scale = 1.0 / math.sqrt(2 * 192 * S * S)
    grad_one[...] = grads[:, :C] * scale
    grad_two[...] = grads[:, C:] * scale


class Mesh:
    def __init__(self):
        self.t = t = lax.axis_index("tile")
        self.b = b = lax.axis_index("batch")
        self.z, self.y, self.x, self.core = z, y, x, core = t // 16, (t // 4) % 4, (t // 2) % 2, t % 2
        self.along_z = [(self.index((z + k) % 4, y, x, core), b) for k in range(1, 4)]
        self.along_y = [(self.index(z, (y + k) % 4, x, core), b) for k in range(1, 4)]
        self.sibling = (self.index(z, y, x, 1 - core), b)
        self.across = (self.index(z, y, 1 - x, core), b)
        self.group = x * 4 + b * 2 + core
        self.near = []
        for k in range(1, 8):
            g = (self.group + k) % 8
            self.near.append((self.index(z, y, g // 4, g % 2), (g // 2) % 2))

    def index(self, z, y, x, core):
        return z * 16 + y * 4 + x * 2 + core

    def greet(self):
        for other in self.along_z + self.along_y + self.near:
            pl.semaphore_signal(
                pltpu.get_barrier_semaphore(), inc=1, device_id=other, device_id_type=MESH
            )

    def meet(self):
        pl.semaphore_wait(pltpu.get_barrier_semaphore(), 13)


class Net:
    def __init__(self, sent, come):
        self.sent, self.come, self.copies = sent, come, []

    def send(self, src, dst, other):
        n = len(self.copies)
        copy = pltpu.make_async_remote_copy(
            src_ref=src, dst_ref=dst, send_sem=self.sent.at[n], recv_sem=self.come.at[n],
            device_id=other, device_id_type=MESH,
        )
        copy.start()
        self.copies.append(copy)
        return copy

    def finish(self):
        for copy in self.copies:
            copy.wait_send()


def find_index(mesh, adjacency, seams, index):
    z, y, x, core = mesh.z, mesh.y, mesh.x, mesh.core

    def decode(device, j):
        tile, code = adjacency[j % 4, device * TL + j // 4], seams[j % 4, device * TL + j // 4]
        source = (tile * 171) >> 9
        return source, (tile - source * 3) * 4 + (code & 3)

    for h in range(2):
        for k in range(4):
            for side in range(2):
                device = (
                    mesh.index(z, (y + k) % 4, side, core) if h == 0 else mesh.index((z + k) % 4, y, side, core)
                )
                for j in range(EDGES):
                    source, line = decode(device, j)
                    p = (source >> 4) if h == 0 else ((source >> 2) & 3)
                    index[(h * 4 + k) * 24 + side * 12 + j] = (p * 2 + (source & 1)) * EDGES + line
    for j in range(EDGES):
        for n, device in enumerate((mesh.index(z, y, 1 - x, core), mesh.t)):
            source, _ = decode(device, j)
            index[192 + n * 24 + j] = ((source >> 2) & 3) * 24
            index[192 + n * 24 + 12 + j] = (source >> 4) * 24
            if n:
                index[240 + j] = (source >> 1) & 1


def exchange_steps(mesh, net, index, x_ref, out_lines, out_corners, refs):
    held_a, held_b, chosen, got_a, got_b, crossing, crossed, cells, apart, ordered = refs
    held, got = (held_a, held_b), (got_a, got_b)
    t, z, y, x, core = mesh.t, mesh.z, mesh.y, mesh.x, mesh.core
    remote, sibling, across = net.send, mesh.sibling, mesh.across
    along_z, along_y = mesh.along_z, mesh.along_y

    chains = ((z, y, along_z, along_y), (y, z, along_y, along_z))
    first, over = [], []
    for h, (p, _, others, _) in enumerate(chains):
        mine = x_ref.at[pl.ds(h * EDGES, EDGES)]
        place = held[h].at[pl.ds((p * 2 + core) * EDGES, EDGES)]
        first.append([remote(mine, place, other) for other in others])
        over.append([remote(mine, place, sibling)])
        held[h][pl.ds((p * 2 + core) * EDGES, EDGES)] = x_ref[pl.ds(h * EDGES, EDGES)]
    cell = ((core * 4 + y) * 4 + z) * 2
    cells[cell + x] = x_ref[2 * EDGES]
    cell_x = remote(x_ref.at[2 * EDGES], cells.at[cell + x], across)
    yield
    for k in range(3):
        for h, (p, _, _, _) in enumerate(chains):
            first[h][k].wait_recv()
            here = held[h].at[pl.ds((((p + 3 - k) % 4) * 2 + core) * EDGES, EDGES)]
            over[h].append(remote(here, here, sibling))
    cell_x.wait_recv()
    here = cells.at[pl.ds(cell, 2)]
    cell_z = [remote(here, here, other) for other in along_z]
    yield

    second = []
    for h, (p, q, _, others) in enumerate(chains):
        for copy in over[h]:
            copy.wait_recv()
        second.append([])
        for k in (1, 2, 3, 0):
            for j in range(2 * EDGES):
                chosen[h, k, j] = held[h][index[(h * 4 + k) * 24 + j]]
            place = got[h].at[pl.ds(q * 2 * EDGES, 2 * EDGES)]
            if k:
                second[h].append(remote(chosen.at[h, k], place, others[k - 1]))
            else:
                got[h][pl.ds(q * 2 * EDGES, 2 * EDGES)] = chosen[h, 0]
    for copy in cell_z:
        copy.wait_recv()
    here = cells.at[pl.ds((core * 4 + y) * 8, 8)]
    cell_y = [remote(here, here, other) for other in along_y]
    yield

    third = []
    for h in range(2):
        for copy in second[h]:
            copy.wait_recv()
        for j in range(EDGES):
            crossing[h, j] = got[h][index[192 + h * 12 + j] + (1 - x) * EDGES + j]
        third.append(remote(crossing.at[h], crossed.at[h], across))
    for copy in cell_y:
        copy.wait_recv()
    here = cells.at[pl.ds(core * 32, 32)]
    last = remote(here, here, sibling)
    yield

    for h in range(2):
        third[h].wait_recv()
        for j in range(EDGES):
            straight = got[h][index[216 + h * 12 + j] + x * EDGES + j]
            near = index[240 + j] == x
            at = slice(j * S + h * HALF, j * S + (h + 1) * HALF)
            out_lines[at, :] = jnp.where(near, straight, crossed[h, j])
    last.wait_recv()
    for d in range(64):
        apart[d * HALF : (d + 1) * HALF, :] = cells[
            (((d % 2) * 4 + (d // 4) % 4) * 4 + d // 16) * 2 + (d // 2) % 2
        ].astype(F32)
    for kind in range(4):
        for tile in range(TL):
            ordered[pl.ds(kind * 256 + tile, 64, stride=TL), :] = apart[
                pl.ds(tile * 4 + kind, 64, stride=HALF), :
            ]
        ordered[pl.ds(kind * 256 + 192, 64), :] = jnp.zeros((64, 128), F32)
    out_corners[...] = ordered[...].astype(BF)
    yield


def total_steps(mesh, net, grads, out_grads, summed, parts, by_y, by_z):
    z, y, group, remote = mesh.z, mesh.y, mesh.group, net.send

    def piece(ref, g):
        return ref.at[pl.ds(pl.multiple_of(g * SHARE, 8), SHARE)]

    scatter = [
        remote(piece(grads, (group + k) % 8), parts.at[group], mesh.near[k - 1]) for k in range(1, 8)
    ]
    parts[group] = grads[pl.ds(pl.multiple_of(group * SHARE, 8), SHARE), :]
    yield
    for copy in scatter:
        copy.wait_recv()
    total = parts[0]
    for g in range(1, 8):
        total = total + parts[g]
    by_y[y] = total
    add_y = [remote(by_y.at[y], by_y.at[y], other) for other in mesh.along_y]
    yield
    for copy in add_y:
        copy.wait_recv()
    by_z[z] = ((by_y[0] + by_y[1]) + by_y[2]) + by_y[3]
    add_z = [remote(by_z.at[z], by_z.at[z], other) for other in mesh.along_z]
    yield
    for copy in add_z:
        copy.wait_recv()
    total = ((by_z[0] + by_z[1]) + by_z[2]) + by_z[3]
    summed[...] = total
    out_grads[pl.ds(pl.multiple_of(group * SHARE, 8), SHARE), :] = total
    gather = [remote(summed, piece(out_grads, group), other) for other in mesh.near]
    yield
    for copy in gather:
        copy.wait_recv()
    yield


ROUND = [
    pltpu.VMEM((8 * EDGES, HALF, 128), BF),
    pltpu.VMEM((8 * EDGES, HALF, 128), BF),
    pltpu.VMEM((2, 4, 2 * EDGES, HALF, 128), BF),
    pltpu.VMEM((8 * EDGES, HALF, 128), BF),
    pltpu.VMEM((8 * EDGES, HALF, 128), BF),
    pltpu.VMEM((2, EDGES, HALF, 128), BF),
    pltpu.VMEM((2, EDGES, HALF, 128), BF),
    pltpu.VMEM((64, HALF, 128), BF),
    pltpu.VMEM((1024, 128), F32),
    pltpu.VMEM((1024, 128), F32),
]
COPIES = 2 * (6 + 2 + 1 + 6 + 3 + 6 + 3 + 2 + 1) + 7 + 3 + 3 + 7


def body(fields, cotangent, first_kernel, second_kernel, adjacency, seam_codes, corner_map):
    f = fields.reshape(R, S * C)
    c = cotangent.reshape(R, S * C)
    tables = (adjacency.T, seam_codes.T, corner_map.T)
    pad, shifts = pltpu.VMEM((PAIRS * PR, 128), F32), pltpu.VMEM((3, PAIRS, R, 128), BF)
    w_conv, w_rim, w_corner = (pltpu.VMEM(shape, BF) for shape in ((3, 512, 256), (384, 256), (128, 512)))
    flat, flat_low = pltpu.VMEM((NP * R, 128), F32), pltpu.VMEM((NP * R, 128), BF)
    turned, shifted, sixteen = (
        pltpu.VMEM((LINES, 128), F32), pltpu.VMEM((LINES, 384), BF), pltpu.VMEM((16, 128), F32),
    )
    quads, kernel = pltpu.VMEM((NP // 2 * R, 256), F32), pltpu.VMEM((3, 3, C, C), F32)
    tile, sums = pltpu.VMEM((R, S * C), BF), pltpu.VMEM((9 * C, 128), F32)
    blocks = pltpu.VMEM((2 * EDGES + 1, HALF, 128), BF)
    near, corners = pltpu.VMEM((LINES, 128), BF), pltpu.VMEM((1024, 128), BF)

    hbm = pl.BlockSpec(memory_space=pltpu.HBM)
    small, small_rows = pltpu.SMEM((4, 192), jnp.int32), pltpu.VMEM((4, 192), jnp.int32)
    corner_rows = pltpu.VMEM((8, 256), jnp.int32)

    def shape(ref):
        return jax.ShapeDtypeStruct(ref.shape, ref.dtype)

    hidden, back, rim, corner, near_two, cells_two, grads = pl.pallas_call(
        first_kernel_body,
        out_shape=tuple(shape(r) for r in (tile, flat, w_rim, w_corner, near, corners, sums)),
        in_specs=[hbm] * 7,
        out_specs=(hbm, hbm) + (VM,) * 5,
        scratch_shapes=[tile, tile, kernel, kernel, small, small, small, small_rows]
        + [pltpu.SemaphoreType.DMA((8,)), pltpu.SemaphoreType.DMA((2,)), corner_rows, tile, flat]
        + [pltpu.SMEM((252,), jnp.int32)]
        + [pad, pad, shifts, shifts, w_conv, w_conv, w_rim, w_corner, turned, shifted, sixteen]
        + [quads, flat, flat, pltpu.VMEM((LINES + HALF, 128), F32), flat_low, flat_low, sums]
        + [blocks, blocks, near, corners]
        + ROUND * 2
        + [pltpu.VMEM((SHARE, 128), F32)]
        + [pltpu.VMEM((k, SHARE, 128), F32) for k in (8, 4, 4)]
        + [pltpu.SemaphoreType.DMA((COPIES,))] * 2,
        name="first",
        compiler_params=pltpu.CompilerParams(
            collective_id=0, has_side_effects=True, vmem_limit_bytes=54 * 2**20
        ),
    )(f, c, first_kernel, second_kernel, *tables)
    kernel_sums = jax.ShapeDtypeStruct((9 * C, C), F32)
    output, field_grad, grad_one, grad_two = pl.pallas_call(
        last_kernel_body,
        out_shape=(shape(tile), shape(tile), kernel_sums, kernel_sums),
        in_specs=[hbm] * 2 + [VM] * 7 + [hbm] * 2 + [VM],
        out_specs=(VM,) * 4,
        scratch_shapes=[tile, flat, small, small, small_rows, pltpu.SemaphoreType.DMA((5,)), corner_rows]
        + [pad, shifts, w_conv, turned, shifted, sixteen, quads],
        name="last",
        compiler_params=pltpu.CompilerParams(vmem_limit_bytes=58 * 2**20),
    )(hidden, back, f, c, second_kernel, rim, corner, near_two, cells_two, *tables[1:], grads)
    shape_out = (1, TL, S, S * C)
    return (
        output.reshape(shape_out),
        field_grad.reshape(shape_out),
        grad_one.reshape(3, 3, C, C),
        grad_two.reshape(3, 3, C, C),
    )


def solution(mesh):
    split = P("batch", "tile", None, None)
    return jax.shard_map(
        body,
        mesh=mesh,
        in_specs=(split, split, P(), P(), P(), P(), P()),
        out_specs=(split, split, P(), P()),
        check_vma=False,
    )
```

time: 71.3 us -> 62.3 us (0.87)
  Pallas kernels: 67.2 us -> 61.4 us
  local copies, waits for them, and re-layouts: 2.31 us -> 0 us
  other arithmetic: 0.8 us -> 0 us
    pallas_call x5 -> x2, Pallas kernels: 67.2 us -> 61.4 us  [the longest x1 55.7 us: body(): pl.pallas_call(first_kernel_body, out_shape=tuple((shape(r) for r in (til...]
    unnamed x9 -> x0, local copies, waits for them, and re-layouts: 1.8 us -> none
    add x1 -> x0, other arithmetic: 0.8 us -> none  [tables(): by_z + by_y * 2 ** 8 + y * 2 ** 16 + z * 2 ** 18 + x * 2 ** 20]
where the time goes in v3:
time: 62.3 us; the launch traced here: 62.1 us
  Pallas kernels  61.4 us (99%)
  between operations  0.64 us (1%)
    pallas_call x1, Pallas kernels, body(): pl.pallas_call(first_kernel_body, out_shape=tuple((shape(r) for r in (til...  55.7 us
    pallas_call x1, Pallas kernels, body(): pl.pallas_call(last_kernel_body, out_shape=(shape(tile), shape(tile), ker...  5.75 us

profile of v3, /device:TPU:1, one launch (start us, length us, event | category | flops | bytes accessed | tf_op | source)
XLA Modules:
  0.0 62.1 jit_solution(5377831623794876087)
XLA Ops:
  0.6 55.7 %first.1 = (bf16[96,2048]{1,0:T(8,128)(2,1)}, f32[1536,128]{1,0:T(8,128)}, bf16[384,256]{1,0:T(8,128)(2,1)}, bf16[128,512]{1,0:T(8,128)(2,1)}, bf16[384,128]{1,0...) custom-call(bf16[96,2048]{1,0:T(8,128)(2,1)} %bitcast.9, bf16[96,2048]{1,0:T(8,128)(2,1)} %bitcast.11, ...), custom_call_target="tpu_custom_call" | custom-call | tf_op jit(solution)/shard_map/first/pallas_call | solution.py:681
  56.3 5.8 %last.1 = (bf16[96,2048]{1,0:T(8,128)(2,1)}, bf16[96,2048]{1,0:T(8,128)(2,1)}, f32[576,64]{1,0:T(8,128)}, f32[576,64]{1,0:T(8,128)}) custom-call(bf16[96,2048]{1,0:T(8,128)(2,1)} %get-tuple-element.15.h_hbm, f32[1536,128]{1,0:T(8,128)} %get-tuple-element.16.back_hbm, bf16[96,2048]{1,0:T(8,128)(2,1)} %bitcast.10, bf16[96,2048]{1,0:T(8,128)(2,1)} %bitcast.12, ...), custom_call_target="tpu_custom_call" | custom-call | tf_op jit(solution)/shard_map/last/pallas_call | solution.py:702

commit v4 on v3

--- a/solution.py
+++ b/solution.py
@@ -21,7 +21,6 @@
 MESH = pl.DeviceIdType.MESH
 F32 = jnp.float32
 BF = jnp.bfloat16
-VM = pl.BlockSpec(memory_space=pltpu.VMEM)
 
 
 def rows_at(t):
@@ -71,6 +70,25 @@
         pad[pl.ds((p + 1) * PR + 120, 8), :] = jnp.zeros((8, 128), F32)
 
 
+def fill_flat(pad, flat, zero):
+    if zero:
+        pad[...] = jnp.zeros_like(pad)
+    for p in range(NP):
+        for t in range(TL):
+            pad[pl.ds(pad_place(p, t), S), :] = flat[pl.ds(flat_place(p, t), S), :]
+
+
+def patch_shifts(xp, pad):
+    for t in range(TL):
+        for p in (0, PAIRS - 1):
+            for a in range(3):
+                xp[a, p, t * S : (t + 1) * S, :] = pad[pl.ds(p * PR + rows_at(t) - 1 + a, S), :].astype(BF)
+        for p in range(1, PAIRS - 1):
+            first = p * PR + rows_at(t)
+            xp[0, p, t * S : t * S + HALF, :] = pad[pl.ds(first - 1, HALF), :].astype(BF)
+            xp[2, p, t * S + HALF : (t + 1) * S, :] = pad[pl.ds(first + HALF + 1, HALF), :].astype(BF)
+
+
 def pad_place(pair, t):
     return (pair + 1) * PR + rows_at(t)
 
@@ -86,19 +104,32 @@
                 xp[a, p, t * S : (t + 1) * S, :] = pad[pl.ds(p * PR + rows_at(t) - 1 + a, S), :].astype(BF)
 
 
-def build_forward(w_out, w):
+def edge_taps(a, c):
+    return [
+        spot for spot in ((0, c), (1, a), (2, c), (3, a)) if (a == 2, c == 0, a == 0, c == 2)[spot[0]]
+    ]
+
+
+def build_forward(w_out, w_edge, w_cell, w):
     w_out[...] = jnp.zeros_like(w_out)
+    w_cell[...] = jnp.zeros_like(w_cell)
     for a in range(3):
         for c in range(3):
             block = w[a, c].astype(BF)
             for n in range(4):
                 m = n + 1 + c
                 w_out[a, m * C : (m + 1) * C, n * C : (n + 1) * C] = block
-
-
-def build_backward(w_out, w_rim, w_corner, w):
+            for e, tap in edge_taps(a, c):
+                w_edge[(2 - tap) * 128 : (2 - tap) * 128 + C, 256 + e * C : 256 + (e + 1) * C] = block
+                w_edge[tap * 128 : tap * 128 + C, 512 + e * C : 512 + (e + 1) * C] = block
+            if a != 1 and c != 1:
+                at = ((a // 2) * 2 + c // 2) * 128
+                w_cell[:C, at : at + C] = block
+                w_cell[:C, at + C : at + 128] = block
+
+
+def build_backward(w_out, w_edge, w_corner, w):
     w_out[...] = jnp.zeros_like(w_out)
-    w_rim[...] = jnp.zeros_like(w_rim)
     w_corner[...] = jnp.zeros_like(w_corner)
     for a in range(3):
         for c in range(3):
@@ -106,21 +137,12 @@
             for n in range(4):
                 m = n + 3 - c
                 w_out[2 - a, m * C : (m + 1) * C, n * C : (n + 1) * C] = block
-            spots = []
-            if a == 2:
-                spots.append((0, c))
-            if c == 0:
-                spots.append((1, a))
-            if a == 0:
-                spots.append((2, c))
-            if c == 2:
-                spots.append((3, a))
-            for e, tap in spots:
-                w_rim[tap * 128 + C : tap * 128 + 128, e * C : (e + 1) * C] = block
+            for e, tap in edge_taps(a, c):
+                w_edge[tap * 128 + C : tap * 128 + 128, e * C : (e + 1) * C] = block
             if a != 1 and c != 1:
-                corner = (a // 2) * 2 + c // 2
-                for half in range(2):
-                    w_corner[C:128, corner * 128 + half * C : corner * 128 + (half + 1) * C] = block
+                at = ((a // 2) * 2 + c // 2) * 128
+                w_corner[C:128, at : at + C] = block
+                w_corner[C:128, at + C : at + 128] = block
 
 
 def conv(xp, w):
@@ -191,34 +213,44 @@
         grad[at, :] = grad[at, :] + jnp.where(upper, part[:C], 0.0)
 
 
-def reverse(kept, codes):
+def reverse(kept, codes, precision=None):
     flip = (
         lax.broadcasted_iota(jnp.int32, (S, S), 0) + lax.broadcasted_iota(jnp.int32, (S, S), 1)
         == S - 1
     )
-    flip = jnp.where(flip, 1.0, 0.0).astype(BF)
-    flipped = jnp.dot(flip, jnp.concatenate(kept, axis=1), preferred_element_type=F32)
+    flip = jnp.where(flip, 1.0, 0.0).astype(kept[0].dtype)
+    flipped = jnp.dot(
+        flip, jnp.concatenate(kept, axis=1), preferred_element_type=F32, precision=precision
+    )
     return [
         jnp.where(codes[j] >= 4, flipped[:, j * 128 : (j + 1) * 128], kept[j].astype(F32))
         for j in range(EDGES)
     ]
 
 
-def orient(lines_ref, codes, w_rim, turned, wide):
+def edge_terms(lines_ref, codes, w_edge, turned, wide, terms):
     lines = lines_ref[...].astype(F32)
     low = low_lanes(S)
     spot = lax.broadcasted_iota(jnp.int32, (LINES, 128), 0) % S
     after = jnp.where(spot == S - 1, 0.0, pltpu.roll(lines, LINES - 1, 0)).astype(BF)
     before = jnp.where(spot == 0, 0.0, pltpu.roll(lines, 1, 0)).astype(BF)
     wide[...] = jnp.concatenate([after, lines_ref[...], before], axis=1)
-    rims = jnp.dot(wide[...], w_rim[...], preferred_element_type=F32)
+    terms[...] = jnp.dot(wide[...], w_edge[...], preferred_element_type=F32)
     kept = []
     for j in range(EDGES):
-        e = codes[j] % 4
-        at = slice(j * S, (j + 1) * S)
-        pair = jnp.where(e >= 2, rims[at, 128:], rims[at, :128])
-        rim = jnp.where(e % 2 == 1, pair, swap(pair))
-        kept.append(jnp.where(low, lines[at], rim).astype(BF))
+        e, at, tile = codes[j] & 3, pl.ds(j * S, S), (j % 4) // 2 * 128
+        pair = jnp.where(e >= 2, terms[at, 128:256], terms[at, :128])
+        rim = jnp.where((e & 1) == 1, pair, swap(pair))
+        halo = jnp.where(
+            codes[j] >= 4, terms[at, 512 + tile : 640 + tile], terms[at, 256 + tile : 384 + tile]
+        )
+        kept.append(jnp.where(low, swap(halo) if j % 2 else halo, rim.astype(BF).astype(F32)))
+    for j, line in enumerate(reverse(kept, codes, lax.Precision.HIGHEST)):
+        turned[pl.ds(j * S, S), :] = line
+
+
+def raw_lines(lines_ref, codes, turned):
+    kept = [lines_ref[pl.ds(j * S, S), :] for j in range(EDGES)]
     for j, line in enumerate(reverse(kept, codes)):
         turned[pl.ds(j * S, S), :] = line
 
@@ -259,26 +291,43 @@
     return total
 
 
-def rims_in(back, turned, sums):
-    low16, low32, low1 = low_lanes(16), low_lanes(S), low_lanes(16)
+def cell_terms(cells, w_cell):
+    every = jnp.dot(cells[...].astype(BF), w_cell[...], preferred_element_type=F32)
+    kind = lax.broadcasted_iota(jnp.int32, (16, 128), 0) % 4
+    total = jnp.zeros((16, 128), F32)
+    for k in range(4):
+        total = jnp.where(kind == k, every[:, k * 128 : (k + 1) * 128], total)
+    return total
+
+
+def add_edges(flat, turned, cells, upper):
+    low16, low32 = low_lanes(16), low_lanes(S)
+
+    def at_low(v):
+        return swap(v) if upper else v
+
+    def at_high(v):
+        return v if upper else swap(v)
+
     for t in range(TL):
         for e, i in ((0, S - 1), (2, 0)):
             base = (t * 4 + e) * S
             even = turned[pl.ds(base, NP, stride=2), :]
             odd = turned[pl.ds(base + 1, NP, stride=2), :]
             at = pl.ds(t * S + i, NP, stride=R)
-            back[at, :] = back[at, :] + jnp.where(low16, swap(even), odd)
+            flat[at, :] = flat[at, :] + jnp.where(low16, at_low(even), at_high(odd))
         at = pl.ds(t * S, S)
-        line = swap(turned[pl.ds((t * 4 + 1) * S, S), :])
-        back[at, :] = back[at, :] + jnp.where(low32, line, 0.0)
+        line = at_low(turned[pl.ds((t * 4 + 1) * S, S), :])
+        flat[at, :] = flat[at, :] + jnp.where(low32, line, 0.0)
         at = pl.ds((NP - 1) * R + t * S, S)
-        back[at, :] = back[at, :] + jnp.where(low32, 0.0, turned[pl.ds((t * 4 + 3) * S, S), :])
-    lows, highs = jnp.where(low1, sums, 0.0), jnp.where(low1, 0.0, sums)
+        line = at_high(turned[pl.ds((t * 4 + 3) * S, S), :])
+        flat[at, :] = flat[at, :] + jnp.where(low32, 0.0, line)
+    lows, highs = jnp.where(low16, cells, 0.0), jnp.where(low16, 0.0, cells)
     for t in range(TL):
         for corner, (i, p) in enumerate(((0, 0), (0, 1), (S - 1, 0), (S - 1, 1))):
             at = pl.ds(p * (NP - 1) * R + t * S + i, 1)
             s = t * 4 + corner
-            back[at, :] = back[at, :] + (highs if p else lows)[s : s + 1]
+            flat[at, :] = flat[at, :] + (highs if p else lows)[s : s + 1]
 
 
 def cells_of(corners_ref, places, me):
@@ -306,13 +355,15 @@
             back[pl.ds((2 * q + half) * R, R), :] = out[q * R : (q + 1) * R, half * 128 : (half + 1) * 128]
 
 
-def first_kernel_body(
+def whole_kernel(
     f_hbm, c_hbm, w1_hbm, w2_hbm, adjacency_hbm, seams_hbm, places_hbm,
-    hidden_hbm, back_hbm, w_rim_two, w_corner_two, near_two, corners_two, out_grads,
-    f_ref, c_ref, w1_ref, w2_ref, adjacency, seams, places, rows, loads, stores, corner_rows,
-    hidden, back_two, index,
-    pad_f, pad_c, xp, qp, w_back, w_forth, w_rim, w_corner, turned, wide, cells, main, back,
-    hid, lines, grads, hids, grad, sent_one, sent_two, near, corners, *refs,
+    output_hbm, field_grad_hbm, grad_one_hbm, grad_two_hbm,
+    f_ref, c_ref, w1_ref, w2_ref, adjacency, seams, places, rows, loads, stores, corner_rows, index,
+    output, field_grad, grad_one, grad_two,
+    pad_f, pad_c, xp, qp, w_forth, w_back, w_forth_two, w_back_two, w_edge, w_edge_two,
+    w_corner, w_cell, w_corner_two, w_cell_two,
+    turned, raw, wide, wide_two, terms, cells, main, back, hid, lines, grads, hids, grad,
+    sent_one, sent_two, near, near_two, corners, corners_two, out_grads, *refs,
 ):
     me = lax.axis_index("tile")
     inputs = [
@@ -345,30 +396,33 @@
     find_index(mesh, adjacency, seams, index)
     load_rows(corner_rows, rows)
     make_shifts(qp, pad_c)
+    make_shifts(xp, pad_f)
+    next(first)
     inputs[2].wait()
-    build_backward(w_back, w_rim, w_corner, w2_ref)
+    inputs[3].wait()
+    w_edge[...] = jnp.zeros_like(w_edge)
+    build_backward(w_back, w_edge, w_corner, w2_ref)
     next(first)
     put_back(back, conv(qp, w_back))
+    build_forward(w_forth, w_edge, w_cell, w1_ref)
+    put_back(main, conv(xp, w_forth))
     next(first)
-    inputs[3].wait()
-    build_forward(w_forth, w1_ref)
+    w_edge_two[...] = jnp.zeros_like(w_edge_two)
+    build_backward(w_back_two, w_edge_two, w_corner_two, w1_ref)
+    build_forward(w_forth_two, w_edge_two, w_cell_two, w2_ref)
     next(first)
-    next(first)
 
     codes = codes_of(seams, me)
-    orient(near, codes, w_rim, turned, wide)
+    edge_terms(near, codes, w_edge, turned, wide, terms)
     cells[...] = cells_of(corners, places, me)
-    halo_in(pad_f, turned, cells)
-    make_shifts(xp, pad_f)
-    rims_in(back, turned, corner_sums(corners, corner_rows, me, w_corner))
-    main[...] = conv(xp, w_forth)
+    add_edges(main, turned, cell_terms(cells, w_cell), False)
+    add_edges(back, turned, corner_sums(corners, corner_rows, me, w_corner), True)
     for p in range(NP):
-        pre = main[pl.ds((p // 2) * R, R), (p % 2) * 128 : (p % 2) * 128 + 128]
         at = pl.ds(p * R, R)
+        pre = main[at, :]
         s = 1.0 / (1.0 + jnp.exp(-pre))
         h = (pre * s).astype(BF)
         g = (back[at, :] * s * (1.0 + pre * (1.0 - s))).astype(BF)
-        hidden[:, p * 128 : (p + 1) * 128] = h
         hid[at, :] = h.astype(F32)
         back[at, :] = g.astype(F32)
         grads[at, :] = g
@@ -376,12 +430,10 @@
     put_lines(lines, hid, back, flat_place, sent_two)
     second = exchange_steps(mesh, net, index, sent_two, near_two, corners_two, two)
     next(second)
-    outputs = [
-        pltpu.make_async_copy(hidden, hidden_hbm, stores.at[0]),
-        pltpu.make_async_copy(back_two, back_hbm, stores.at[1]),
-    ]
-    outputs[0].start()
-
+
+    raw_lines(near, codes, raw)
+    halo_in(pad_f, raw, cells)
+    patch_shifts(xp, pad_f)
     low = low_lanes(192)
     for a in range(3):
         grad[pl.ds(a * 192, 192), :] = jnp.where(
@@ -391,61 +443,60 @@
     adding = total_steps(mesh, net, grad, out_grads, summed, parts, by_y, by_z)
     next(adding)
     next(second)
-    for p in range(NP):
-        for t in range(TL):
-            pad_c[pl.ds(pad_place(p, t), S), :] = back[pl.ds(flat_place(p, t), S), :]
-    build_backward(w_back, w_rim_two, w_corner_two, w1_ref)
+    fill_flat(pad_f, hid, True)
     next(second)
+    make_shifts(xp, pad_f)
+    put_back(main, conv(xp, w_forth_two))
+    next(adding)
+    fill_flat(pad_c, back, False)
     make_shifts(qp, pad_c)
-    next(adding)
-    put_back(back_two, conv(qp, w_back))
-    outputs[1].start()
-    next(second)
-    next(adding)
+    put_back(back, conv(qp, w_back_two))
     next(adding)
     next(second)
     next(adding)
-    net.finish()
-    for copy in outputs:
-        copy.wait()
-
-
-def last_kernel_body(
-    h_hbm, back_hbm, f_ref, c_ref, w2_ref, w_rim, w_corner, near, corners, seams_hbm, places_hbm, grads,
-    output, field_grad, grad_one, grad_two,
-    h_ref, back, seams, places, rows, loads, corner_rows, pad, xp, w_forth, turned, wide, cells, main,
-):
-    me = lax.axis_index("tile")
-    inputs = [
-        pltpu.make_async_copy(src, dst, loads.at[n])
+    next(second)
+
+    edge_terms(near_two, codes, w_edge_two, turned, wide_two, terms)
+    cells[...] = cells_of(corners_two, places, me)
+    add_edges(main, turned, cell_terms(cells, w_cell_two), False)
+    add_edges(back, turned, corner_sums(corners_two, corner_rows, me, w_corner_two), True)
+    for p in range(NP):
+        at, lanes = pl.ds(p * R, R), slice(p * 128, (p + 1) * 128)
+        output[:, lanes] = (f_ref[:, lanes].astype(F32) + main[at, :]).astype(BF)
+        field_grad[:, lanes] = (c_ref[:, lanes].astype(F32) + back[at, :]).astype(BF)
+    results = [
+        pltpu.make_async_copy(src, dst, stores.at[n])
         for n, (src, dst) in enumerate(
             (
-                (seams_hbm, seams), (places_hbm, places), (places_hbm, rows), (h_hbm, h_ref),
-                (back_hbm, back),
+                (output, output_hbm), (field_grad, field_grad_hbm),
+                (grad_one, grad_one_hbm), (grad_two, grad_two_hbm),
             )
         )
     ]
-    for copy in inputs:
+    results[0].start()
+    results[1].start()
+    next(adding)
+    scale = 1.0 / math.sqrt(2 * 192 * S * S)
+    grad_one[...] = out_grads[:, :C] * scale
+    grad_two[...] = out_grads[:, C:] * scale
+    results[2].start()
+    results[3].start()
+    net.finish()
+    for copy in results:
+        copy.wait()
+
+
+def hand_over(*refs):
+    ins, outs, held, come, gone = refs[:4], refs[4:8], refs[8:12], refs[12], refs[13]
+    arrive = [pltpu.make_async_copy(a, b, come.at[n]) for n, (a, b) in enumerate(zip(ins, held))]
+    leave = [pltpu.make_async_copy(a, b, gone.at[n]) for n, (a, b) in enumerate(zip(held, outs))]
+    for copy in arrive:
         copy.start()
-    build_forward(w_forth, w2_ref)
-    for copy in inputs:
+    for n in range(4):
+        arrive[n].wait()
+        leave[n].start()
+    for copy in leave:
         copy.wait()
-    load_rows(corner_rows, rows)
-    orient(near, codes_of(seams, me), w_rim, turned, wide)
-    cells[...] = cells_of(corners, places, me)
-    fill_pad(pad, h_ref)
-    halo_in(pad, turned, cells)
-    make_shifts(xp, pad)
-    main[...] = conv(xp, w_forth)
-    rims_in(back, turned, corner_sums(corners, corner_rows, me, w_corner))
-    for p in range(NP):
-        at, lanes = pl.ds(p * R, R), slice(p * 128, (p + 1) * 128)
-        made = main[pl.ds((p // 2) * R, R), (p % 2) * 128 : (p % 2) * 128 + 128]
-        output[:, lanes] = (f_ref[:, lanes].astype(F32) + made).astype(BF)
-        field_grad[:, lanes] = (c_ref[:, lanes].astype(F32) + back[at, :]).astype(BF)
-    scale = 1.0 / math.sqrt(2 * 192 * S * S)
-    grad_one[...] = grads[:, :C] * scale
-    grad_two[...] = grads[:, C:] * scale
 
 
 class Mesh:
@@ -661,54 +712,50 @@
     c = cotangent.reshape(R, S * C)
     tables = (adjacency.T, seam_codes.T, corner_map.T)
     pad, shifts = pltpu.VMEM((PAIRS * PR, 128), F32), pltpu.VMEM((3, PAIRS, R, 128), BF)
-    w_conv, w_rim, w_corner = (pltpu.VMEM(shape, BF) for shape in ((3, 512, 256), (384, 256), (128, 512)))
+    w_conv, w_edge = pltpu.VMEM((3, 512, 256), BF), pltpu.VMEM((384, 768), BF)
+    w_corner = pltpu.VMEM((128, 512), BF)
     flat, flat_low = pltpu.VMEM((NP * R, 128), F32), pltpu.VMEM((NP * R, 128), BF)
-    turned, shifted, sixteen = (
-        pltpu.VMEM((LINES, 128), F32), pltpu.VMEM((LINES, 384), BF), pltpu.VMEM((16, 128), F32),
-    )
-    quads, kernel = pltpu.VMEM((NP // 2 * R, 256), F32), pltpu.VMEM((3, 3, C, C), F32)
+    turned, shifted = pltpu.VMEM((LINES, 128), F32), pltpu.VMEM((LINES, 384), BF)
+    terms, sixteen = pltpu.VMEM((LINES, 768), F32), pltpu.VMEM((16, 128), F32)
+    kernel, kernel_sum = pltpu.VMEM((3, 3, C, C), F32), pltpu.VMEM((9 * C, C), F32)
     tile, sums = pltpu.VMEM((R, S * C), BF), pltpu.VMEM((9 * C, 128), F32)
     blocks = pltpu.VMEM((2 * EDGES + 1, HALF, 128), BF)
     near, corners = pltpu.VMEM((LINES, 128), BF), pltpu.VMEM((1024, 128), BF)
-
     hbm = pl.BlockSpec(memory_space=pltpu.HBM)
-    small, small_rows = pltpu.SMEM((4, 192), jnp.int32), pltpu.VMEM((4, 192), jnp.int32)
-    corner_rows = pltpu.VMEM((8, 256), jnp.int32)
-
-    def shape(ref):
-        return jax.ShapeDtypeStruct(ref.shape, ref.dtype)
-
-    hidden, back, rim, corner, near_two, cells_two, grads = pl.pallas_call(
-        first_kernel_body,
-        out_shape=tuple(shape(r) for r in (tile, flat, w_rim, w_corner, near, corners, sums)),
+    small = pltpu.SMEM((4, 192), jnp.int32)
+    sem = pltpu.SemaphoreType.DMA
+    shapes = tuple(jax.ShapeDtypeStruct(r.shape, r.dtype) for r in (tile, tile, kernel_sum, kernel_sum))
+    results = pl.pallas_call(
+        whole_kernel,
+        out_shape=shapes,
         in_specs=[hbm] * 7,
-        out_specs=(hbm, hbm) + (VM,) * 5,
-        scratch_shapes=[tile, tile, kernel, kernel, small, small, small, small_rows]
-        + [pltpu.SemaphoreType.DMA((8,)), pltpu.SemaphoreType.DMA((2,)), corner_rows, tile, flat]
-        + [pltpu.SMEM((252,), jnp.int32)]
-        + [pad, pad, shifts, shifts, w_conv, w_conv, w_rim, w_corner, turned, shifted, sixteen]
-        + [quads, flat, flat, pltpu.VMEM((LINES + HALF, 128), F32), flat_low, flat_low, sums]
-        + [blocks, blocks, near, corners]
+        out_specs=(hbm,) * 4,
+        scratch_shapes=[tile, tile, kernel, kernel, small, small, small]
+        + [pltpu.VMEM((4, 192), jnp.int32), sem((8,)), sem((4,)), pltpu.VMEM((8, 256), jnp.int32)]
+        + [pltpu.SMEM((252,), jnp.int32), tile, tile, kernel_sum, kernel_sum]
+        + [pad, pad, shifts, shifts, w_conv, w_conv, w_conv, w_conv, w_edge, w_edge]
+        + [w_corner] * 4
+        + [turned, turned, shifted, shifted, terms, sixteen, flat, flat, flat]
+        + [pltpu.VMEM((LINES + HALF, 128), F32), flat_low, flat_low, sums]
+        + [blocks, blocks, near, near, corners, corners, sums]
         + ROUND * 2
         + [pltpu.VMEM((SHARE, 128), F32)]
         + [pltpu.VMEM((k, SHARE, 128), F32) for k in (8, 4, 4)]
-        + [pltpu.SemaphoreType.DMA((COPIES,))] * 2,
-        name="first",
+        + [sem((COPIES,))] * 2,
+        name="whole",
         compiler_params=pltpu.CompilerParams(
             collective_id=0, has_side_effects=True, vmem_limit_bytes=54 * 2**20
         ),
     )(f, c, first_kernel, second_kernel, *tables)
-    kernel_sums = jax.ShapeDtypeStruct((9 * C, C), F32)
     output, field_grad, grad_one, grad_two = pl.pallas_call(
-        last_kernel_body,
-        out_shape=(shape(tile), shape(tile), kernel_sums, kernel_sums),
-        in_specs=[hbm] * 2 + [VM] * 7 + [hbm] * 2 + [VM],
-        out_specs=(VM,) * 4,
-        scratch_shapes=[tile, flat, small, small, small_rows, pltpu.SemaphoreType.DMA((5,)), corner_rows]
-        + [pad, shifts, w_conv, turned, shifted, sixteen, quads],
-        name="last",
+        hand_over,
+        out_shape=shapes,
+        in_specs=[hbm] * 4,
+        out_specs=(hbm,) * 4,
+        scratch_shapes=[tile, tile, kernel_sum, kernel_sum, sem((4,)), sem((4,))],
+        name="hand_over",
         compiler_params=pltpu.CompilerParams(vmem_limit_bytes=58 * 2**20),
-    )(hidden, back, f, c, second_kernel, rim, corner, near_two, cells_two, *tables[1:], grads)
+    )(*results)
     shape_out = (1, TL, S, S * C)
     return (
         output.reshape(shape_out),

time: 62.3 us -> 57.4 us (0.921)
  Pallas kernels: 61.4 us -> 56.6 us
    pallas_call x2, Pallas kernels: 61.4 us -> 56.6 us  [the longest x1 54.5 us: body(): pl.pallas_call(whole_kernel, out_shape=shapes, in_specs=[hbm] * 7, out_sp...]
where the time goes in v4:
time: 57.4 us; the launch traced here: 57.2 us
  Pallas kernels  56.6 us (99%)
  between operations  0.64 us (1%)
    pallas_call x1, Pallas kernels, body(): pl.pallas_call(whole_kernel, out_shape=shapes, in_specs=[hbm] * 7, out_sp...  54.5 us
    pallas_call x1, Pallas kernels, body(): pl.pallas_call(hand_over, out_shape=shapes, in_specs=[hbm] * 4, out_specs...  2.14 us

profile of v4, /device:TPU:1, one launch (start us, length us, event | category | flops | bytes accessed | tf_op | source)
XLA Modules:
  0.0 57.2 jit_solution(3366790279045849053)
XLA Ops:
  0.6 54.5 %whole.1 = (bf16[96,2048]{1,0:T(8,128)(2,1)}, bf16[96,2048]{1,0:T(8,128)(2,1)}, f32[576,64]{1,0:T(8,128)}, f32[576,64]{1,0:T(8,128)}) custom-call(bf16[96,2048]{1,0:T(8,128)(2,1)} %bitcast.9, bf16[96,2048]{1,0:T(8,128)(2,1)} %bitcast.10, f32[3,3,64,64]{3,2,1,0:T(8,128)} %w1_hbm.1, f32[3,3,64,64]{3,2,1,0:T(8,128)} %w2_hbm.1, s32[4,192]{1,0:T(4,128)} %bitcast.11, ...), custom_call_target="tpu_custom_call" | custom-call | tf_op jit(solution)/shard_map/whole/pallas_call | solution.py:728
  55.1 2.1 %hand_over.1 = (bf16[96,2048]{1,0:T(8,128)(2,1)}, bf16[96,2048]{1,0:T(8,128)(2,1)}, f32[576,64]{1,0:T(8,128)}, f32[576,64]{1,0:T(8,128)}) custom-call(bf16[96,2048]{1,0:T(8,128)(2,1)} %get-tuple-element.12.refs_0_, bf16[96,2048]{1,0:T(8,128)(2,1)} %get-tuple-element.13.refs_1_, f32[576,64]{1,0:T(8,128)} %get-tuple-element.14.refs_2_, ...), custom_call_target="tpu_custom_call" | custom-call | tf_op jit(solution)/shard_map/hand_over/pallas_call | solution.py:750

commit v5 on v4

--- a/solution.py
+++ b/solution.py
@@ -300,7 +300,7 @@
     return total
 
 
-def add_edges(flat, turned, cells, upper):
+def add_edges(flat, turned, upper):
     low16, low32 = low_lanes(16), low_lanes(S)
 
     def at_low(v):
@@ -322,6 +322,10 @@
         at = pl.ds((NP - 1) * R + t * S, S)
         line = at_high(turned[pl.ds((t * 4 + 3) * S, S), :])
         flat[at, :] = flat[at, :] + jnp.where(low32, 0.0, line)
+
+
+def add_cells(flat, cells):
+    low16 = low_lanes(16)
     lows, highs = jnp.where(low16, cells, 0.0), jnp.where(low16, 0.0, cells)
     for t in range(TL):
         for corner, (i, p) in enumerate(((0, 0), (0, 1), (S - 1, 0), (S - 1, 1))):
@@ -396,27 +400,30 @@
     find_index(mesh, adjacency, seams, index)
     load_rows(corner_rows, rows)
     make_shifts(qp, pad_c)
-    make_shifts(xp, pad_f)
     next(first)
     inputs[2].wait()
     inputs[3].wait()
+    make_shifts(xp, pad_f)
     w_edge[...] = jnp.zeros_like(w_edge)
     build_backward(w_back, w_edge, w_corner, w2_ref)
+    next(first)
     next(first)
     put_back(back, conv(qp, w_back))
     build_forward(w_forth, w_edge, w_cell, w1_ref)
     put_back(main, conv(xp, w_forth))
-    next(first)
     w_edge_two[...] = jnp.zeros_like(w_edge_two)
     build_backward(w_back_two, w_edge_two, w_corner_two, w1_ref)
     build_forward(w_forth_two, w_edge_two, w_cell_two, w2_ref)
     next(first)
+    cells[...] = cells_of(corners, places, me)
+    add_cells(main, cell_terms(cells, w_cell))
+    add_cells(back, corner_sums(corners, corner_rows, me, w_corner))
+    next(first)
 
     codes = codes_of(seams, me)
     edge_terms(near, codes, w_edge, turned, wide, terms)
-    cells[...] = cells_of(corners, places, me)
-    add_edges(main, turned, cell_terms(cells, w_cell), False)
-    add_edges(back, turned, corner_sums(corners, corner_rows, me, w_corner), True)
+    add_edges(main, turned, False)
+    add_edges(back, turned, True)
     for p in range(NP):
         at = pl.ds(p * R, R)
         pre = main[at, :]
@@ -444,22 +451,25 @@
     next(adding)
     next(second)
     fill_flat(pad_f, hid, True)
-    next(second)
     make_shifts(xp, pad_f)
-    put_back(main, conv(xp, w_forth_two))
-    next(adding)
-    fill_flat(pad_c, back, False)
-    make_shifts(qp, pad_c)
-    put_back(back, conv(qp, w_back_two))
-    next(adding)
     next(second)
     next(adding)
     next(second)
+    put_back(main, conv(xp, w_forth_two))
+    fill_flat(pad_c, back, False)
+    make_shifts(qp, pad_c)
+    next(adding)
+    put_back(back, conv(qp, w_back_two))
+    next(second)
+    cells[...] = cells_of(corners_two, places, me)
+    add_cells(main, cell_terms(cells, w_cell_two))
+    add_cells(back, corner_sums(corners_two, corner_rows, me, w_corner_two))
+    next(adding)
+    next(second)
 
     edge_terms(near_two, codes, w_edge_two, turned, wide_two, terms)
-    cells[...] = cells_of(corners_two, places, me)
-    add_edges(main, turned, cell_terms(cells, w_cell_two), False)
-    add_edges(back, turned, corner_sums(corners_two, corner_rows, me, w_corner_two), True)
+    add_edges(main, turned, False)
+    add_edges(back, turned, True)
     for p in range(NP):
         at, lanes = pl.ds(p * R, R), slice(p * 128, (p + 1) * 128)
         output[:, lanes] = (f_ref[:, lanes].astype(F32) + main[at, :]).astype(BF)
@@ -556,50 +566,65 @@
 
     for h in range(2):
         for k in range(4):
-            for side in range(2):
-                device = (
-                    mesh.index(z, (y + k) % 4, side, core) if h == 0 else mesh.index((z + k) % 4, y, side, core)
-                )
-                for j in range(EDGES):
-                    source, line = decode(device, j)
-                    p = (source >> 4) if h == 0 else ((source >> 2) & 3)
-                    index[(h * 4 + k) * 24 + side * 12 + j] = (p * 2 + (source & 1)) * EDGES + line
-    for j in range(EDGES):
-        for n, device in enumerate((mesh.index(z, y, 1 - x, core), mesh.t)):
-            source, _ = decode(device, j)
-            index[192 + n * 24 + j] = ((source >> 2) & 3) * 24
-            index[192 + n * 24 + 12 + j] = (source >> 4) * 24
-            if n:
-                index[240 + j] = (source >> 1) & 1
+            device = mesh.index(z, (y + k) % 4, x, core) if h == 0 else mesh.index((z + k) % 4, y, x, core)
+            for j in range(EDGES):
+                source, line = decode(device, j)
+                p = (source >> 4) if h == 0 else ((source >> 2) & 3)
+                index[(h * 4 + k) * 12 + j] = (p * 4 + (source & 3)) * EDGES + line
+                if k == 0:
+                    q = ((source >> 2) & 3) if h == 0 else (source >> 4)
+                    index[96 + h * 12 + j] = q * EDGES + j
 
 
 def exchange_steps(mesh, net, index, x_ref, out_lines, out_corners, refs):
-    held_a, held_b, chosen, got_a, got_b, crossing, crossed, cells, apart, ordered = refs
+    held_a, held_b, chosen, got_a, got_b, cells, apart, ordered = refs
     held, got = (held_a, held_b), (got_a, got_b)
-    t, z, y, x, core = mesh.t, mesh.z, mesh.y, mesh.x, mesh.core
+    z, y, x, core = mesh.z, mesh.y, mesh.x, mesh.core
     remote, sibling, across = net.send, mesh.sibling, mesh.across
     along_z, along_y = mesh.along_z, mesh.along_y
-
     chains = ((z, y, along_z, along_y), (y, z, along_y, along_z))
-    first, over = [], []
+
+    def place(h, p, side):
+        return held[h].at[pl.ds((p * 4 + side * 2 + core) * EDGES, EDGES)]
+
+    first, over, passed, turn = [], [], [], []
+    cell = ((core * 4 + y) * 4 + z) * 2
+    for h, (p, _, _, _) in enumerate(chains):
+        turn.append(remote(x_ref.at[pl.ds(h * EDGES, EDGES)], place(h, p, x), across))
+    cell_x = remote(x_ref.at[2 * EDGES], cells.at[cell + x], across)
     for h, (p, _, others, _) in enumerate(chains):
         mine = x_ref.at[pl.ds(h * EDGES, EDGES)]
-        place = held[h].at[pl.ds((p * 2 + core) * EDGES, EDGES)]
-        first.append([remote(mine, place, other) for other in others])
-        over.append([remote(mine, place, sibling)])
-        held[h][pl.ds((p * 2 + core) * EDGES, EDGES)] = x_ref[pl.ds(h * EDGES, EDGES)]
-    cell = ((core * 4 + y) * 4 + z) * 2
+        first.append([remote(mine, place(h, p, x), other) for other in others])
+    for h, (p, _, _, _) in enumerate(chains):
+        over.append([remote(x_ref.at[pl.ds(h * EDGES, EDGES)], place(h, p, x), sibling)])
+        held[h][pl.ds((p * 4 + x * 2 + core) * EDGES, EDGES)] = x_ref[pl.ds(h * EDGES, EDGES)]
     cells[cell + x] = x_ref[2 * EDGES]
-    cell_x = remote(x_ref.at[2 * EDGES], cells.at[cell + x], across)
-    yield
-    for k in range(3):
-        for h, (p, _, _, _) in enumerate(chains):
-            first[h][k].wait_recv()
-            here = held[h].at[pl.ds((((p + 3 - k) % 4) * 2 + core) * EDGES, EDGES)]
-            over[h].append(remote(here, here, sibling))
+    yield
+
+    for h, (p, _, others, _) in enumerate(chains):
+        turn[h].wait_recv()
+        here = place(h, p, 1 - x)
+        passed.append([remote(here, here, other) for other in others])
+        over[h].append(remote(here, here, sibling))
     cell_x.wait_recv()
     here = cells.at[pl.ds(cell, 2)]
     cell_z = [remote(here, here, other) for other in along_z]
+    for k in (0, 2, 1):
+        for h, (p, _, _, _) in enumerate(chains):
+            first[h][k].wait_recv()
+            here = place(h, (p + 3 - k) % 4, x)
+            over[h].append(remote(here, here, sibling))
+    yield
+
+    for copy in cell_z:
+        copy.wait_recv()
+    here = cells.at[pl.ds((core * 4 + y) * 8, 8)]
+    cell_y = [remote(here, here, other) for other in along_y]
+    for k in (0, 2, 1):
+        for h, (p, _, _, _) in enumerate(chains):
+            passed[h][k].wait_recv()
+            here = place(h, (p + 3 - k) % 4, 1 - x)
+            over[h].append(remote(here, here, sibling))
     yield
 
     second = []
@@ -607,40 +632,20 @@
         for copy in over[h]:
             copy.wait_recv()
         second.append([])
-        for k in (1, 2, 3, 0):
-            for j in range(2 * EDGES):
-                chosen[h, k, j] = held[h][index[(h * 4 + k) * 24 + j]]
-            place = got[h].at[pl.ds(q * 2 * EDGES, 2 * EDGES)]
+        for k in (2, 1, 3, 0):
+            for j in range(EDGES):
+                chosen[h, k, j] = held[h][index[(h * 4 + k) * 12 + j]]
             if k:
-                second[h].append(remote(chosen.at[h, k], place, others[k - 1]))
+                there = got[h].at[pl.ds(q * EDGES, EDGES)]
+                second[h].append(remote(chosen.at[h, k], there, others[k - 1]))
             else:
-                got[h][pl.ds(q * 2 * EDGES, 2 * EDGES)] = chosen[h, 0]
-    for copy in cell_z:
-        copy.wait_recv()
-    here = cells.at[pl.ds((core * 4 + y) * 8, 8)]
-    cell_y = [remote(here, here, other) for other in along_y]
-    yield
-
-    third = []
-    for h in range(2):
-        for copy in second[h]:
-            copy.wait_recv()
-        for j in range(EDGES):
-            crossing[h, j] = got[h][index[192 + h * 12 + j] + (1 - x) * EDGES + j]
-        third.append(remote(crossing.at[h], crossed.at[h], across))
+                got[h][pl.ds(q * EDGES, EDGES)] = chosen[h, 0]
     for copy in cell_y:
         copy.wait_recv()
     here = cells.at[pl.ds(core * 32, 32)]
     last = remote(here, here, sibling)
     yield
 
-    for h in range(2):
-        third[h].wait_recv()
-        for j in range(EDGES):
-            straight = got[h][index[216 + h * 12 + j] + x * EDGES + j]
-            near = index[240 + j] == x
-            at = slice(j * S + h * HALF, j * S + (h + 1) * HALF)
-            out_lines[at, :] = jnp.where(near, straight, crossed[h, j])
     last.wait_recv()
     for d in range(64):
         apart[d * HALF : (d + 1) * HALF, :] = cells[
@@ -655,6 +660,13 @@
     out_corners[...] = ordered[...].astype(BF)
     yield
 
+    for h in range(2):
+        for copy in second[h]:
+            copy.wait_recv()
+        for j in range(EDGES):
+            out_lines[j * S + h * HALF : j * S + (h + 1) * HALF, :] = got[h][index[96 + h * 12 + j]]
+    yield
+
 
 def total_steps(mesh, net, grads, out_grads, summed, parts, by_y, by_z):
     z, y, group, remote = mesh.z, mesh.y, mesh.group, net.send
@@ -693,18 +705,16 @@
 
 
 ROUND = [
-    pltpu.VMEM((8 * EDGES, HALF, 128), BF),
-    pltpu.VMEM((8 * EDGES, HALF, 128), BF),
-    pltpu.VMEM((2, 4, 2 * EDGES, HALF, 128), BF),
-    pltpu.VMEM((8 * EDGES, HALF, 128), BF),
-    pltpu.VMEM((8 * EDGES, HALF, 128), BF),
-    pltpu.VMEM((2, EDGES, HALF, 128), BF),
-    pltpu.VMEM((2, EDGES, HALF, 128), BF),
+    pltpu.VMEM((16 * EDGES, HALF, 128), BF),
+    pltpu.VMEM((16 * EDGES, HALF, 128), BF),
+    pltpu.VMEM((2, 4, EDGES, HALF, 128), BF),
+    pltpu.VMEM((4 * EDGES, HALF, 128), BF),
+    pltpu.VMEM((4 * EDGES, HALF, 128), BF),
     pltpu.VMEM((64, HALF, 128), BF),
     pltpu.VMEM((1024, 128), F32),
     pltpu.VMEM((1024, 128), F32),
 ]
-COPIES = 2 * (6 + 2 + 1 + 6 + 3 + 6 + 3 + 2 + 1) + 7 + 3 + 3 + 7
+COPIES = 2 * (2 + 1 + 6 + 2 + 6 + 2 + 3 + 6 + 3 + 6 + 6 + 1) + 7 + 3 + 3 + 7
 
 
 def body(fields, cotangent, first_kernel, second_kernel, adjacency, seam_codes, corner_map):
@@ -732,7 +742,7 @@
         out_specs=(hbm,) * 4,
         scratch_shapes=[tile, tile, kernel, kernel, small, small, small]
         + [pltpu.VMEM((4, 192), jnp.int32), sem((8,)), sem((4,)), pltpu.VMEM((8, 256), jnp.int32)]
-        + [pltpu.SMEM((252,), jnp.int32), tile, tile, kernel_sum, kernel_sum]
+        + [pltpu.SMEM((120,), jnp.int32), tile, tile, kernel_sum, kernel_sum]
         + [pad, pad, shifts, shifts, w_conv, w_conv, w_conv, w_conv, w_edge, w_edge]
         + [w_corner] * 4
         + [turned, turned, shifted, shifted, terms, sixteen, flat, flat, flat]

time: 57.4 us -> 53.3 us (0.929)
  Pallas kernels: 56.6 us -> 52.5 us
    pallas_call x1, Pallas kernels: 54.5 us -> 50.4 us  [body(): pl.pallas_call(whole_kernel, out_shape=shapes, in_specs=[hbm] * 7, out_sp...]
where the time goes in v5:
time: 53.3 us; the launch traced here: 53.2 us
  Pallas kernels  52.5 us (98%)
  between operations  0.64 us (1%)
    pallas_call x1, Pallas kernels, body(): pl.pallas_call(whole_kernel, out_shape=shapes, in_specs=[hbm] * 7, out_sp...  50.4 us
    pallas_call x1, Pallas kernels, body(): pl.pallas_call(hand_over, out_shape=shapes, in_specs=[hbm] * 4, out_specs...  2.14 us

profile of v5, /device:TPU:1, one launch (start us, length us, event | category | flops | bytes accessed | tf_op | source)
XLA Modules:
  0.0 53.2 jit_solution(4344289758422473186)
XLA Ops:
  0.6 50.4 %whole.1 = (bf16[96,2048]{1,0:T(8,128)(2,1)}, bf16[96,2048]{1,0:T(8,128)(2,1)}, f32[576,64]{1,0:T(8,128)}, f32[576,64]{1,0:T(8,128)}) custom-call(bf16[96,2048]{1,0:T(8,128)(2,1)} %bitcast.9, bf16[96,2048]{1,0:T(8,128)(2,1)} %bitcast.10, f32[3,3,64,64]{3,2,1,0:T(8,128)} %w1_hbm.1, f32[3,3,64,64]{3,2,1,0:T(8,128)} %w2_hbm.1, s32[4,192]{1,0:T(4,128)} %bitcast.11, ...), custom_call_target="tpu_custom_call" | custom-call | tf_op jit(solution)/shard_map/whole/pallas_call | solution.py:738
  51.0 2.1 %hand_over.1 = (bf16[96,2048]{1,0:T(8,128)(2,1)}, bf16[96,2048]{1,0:T(8,128)(2,1)}, f32[576,64]{1,0:T(8,128)}, f32[576,64]{1,0:T(8,128)}) custom-call(bf16[96,2048]{1,0:T(8,128)(2,1)} %get-tuple-element.12.refs_0_, bf16[96,2048]{1,0:T(8,128)(2,1)} %get-tuple-element.13.refs_1_, f32[576,64]{1,0:T(8,128)} %get-tuple-element.14.refs_2_, ...), custom_call_target="tpu_custom_call" | custom-call | tf_op jit(solution)/shard_map/hand_over/pallas_call | solution.py:760

commit v6 on v5

--- a/solution.py
+++ b/solution.py
@@ -385,7 +385,7 @@
     mesh.greet()
     n = len(ROUND)
     one, two, rest = refs[:n], refs[n : 2 * n], refs[2 * n :]
-    summed, parts, by_y, by_z, sent, come = rest
+    summed, parts, by_y, by_z, leaving, sent, come = rest
     net = Net(sent, come)
     inputs[0].wait()
     fill_pad(pad_f, f_ref)
@@ -395,19 +395,17 @@
     mesh.meet()
     first = exchange_steps(mesh, net, index, sent_one, near, corners, one)
     next(first)
-    for copy in inputs[4:]:
+    for copy in inputs[2:]:
         copy.wait()
+    make_shifts(qp, pad_c)
+    next(first)
     find_index(mesh, adjacency, seams, index)
     load_rows(corner_rows, rows)
-    make_shifts(qp, pad_c)
     next(first)
-    inputs[2].wait()
-    inputs[3].wait()
+    w_edge[...] = jnp.zeros_like(w_edge)
+    next(first)
     make_shifts(xp, pad_f)
-    w_edge[...] = jnp.zeros_like(w_edge)
     build_backward(w_back, w_edge, w_corner, w2_ref)
-    next(first)
-    next(first)
     put_back(back, conv(qp, w_back))
     build_forward(w_forth, w_edge, w_cell, w1_ref)
     put_back(main, conv(xp, w_forth))
@@ -436,7 +434,9 @@
         hids[at, :] = h
     put_lines(lines, hid, back, flat_place, sent_two)
     second = exchange_steps(mesh, net, index, sent_two, near_two, corners_two, two)
+    sofar = len(net.copies)
     next(second)
+    net.drain(sofar)
 
     raw_lines(near, codes, raw)
     halo_in(pad_f, raw, cells)
@@ -447,24 +447,26 @@
             low, first_part(xp, grads[...], a), second_part(qp, hids[...], a)
         )
     second_rims(grad, lines, wide, corners, corner_rows, codes, me)
-    adding = total_steps(mesh, net, grad, out_grads, summed, parts, by_y, by_z)
+    adding = total_steps(mesh, net, grad, out_grads, summed, parts, by_y, by_z, leaving)
     next(adding)
     next(second)
     fill_flat(pad_f, hid, True)
     make_shifts(xp, pad_f)
-    next(second)
     next(adding)
     next(second)
     put_back(main, conv(xp, w_forth_two))
+    next(second)
+    next(adding)
     fill_flat(pad_c, back, False)
     make_shifts(qp, pad_c)
+    put_back(back, conv(qp, w_back_two))
+    sofar = len(net.copies)
     next(adding)
-    put_back(back, conv(qp, w_back_two))
+    net.drain(sofar)
     next(second)
     cells[...] = cells_of(corners_two, places, me)
     add_cells(main, cell_terms(cells, w_cell_two))
     add_cells(back, corner_sums(corners_two, corner_rows, me, w_corner_two))
-    next(adding)
     next(second)
 
     edge_terms(near_two, codes, w_edge_two, turned, wide_two, terms)
@@ -487,11 +489,13 @@
     results[1].start()
     next(adding)
     scale = 1.0 / math.sqrt(2 * 192 * S * S)
-    grad_one[...] = out_grads[:, :C] * scale
-    grad_two[...] = out_grads[:, C:] * scale
+    for g in range(8):
+        share = out_grads[g].astype(F32)[:SHARE] * scale
+        grad_one[pl.ds(g * SHARE, SHARE), :] = share[:, :C]
+        grad_two[pl.ds(g * SHARE, SHARE), :] = share[:, C:]
     results[2].start()
     results[3].start()
-    net.finish()
+    net.drain()
     for copy in results:
         copy.wait()
 
@@ -539,7 +543,7 @@
 
 class Net:
     def __init__(self, sent, come):
-        self.sent, self.come, self.copies = sent, come, []
+        self.sent, self.come, self.copies, self.waited = sent, come, [], 0
 
     def send(self, src, dst, other):
         n = len(self.copies)
@@ -551,9 +555,11 @@
         self.copies.append(copy)
         return copy
 
-    def finish(self):
-        for copy in self.copies:
+    def drain(self, stop=None):
+        stop = len(self.copies) if stop is None else stop
+        for copy in self.copies[self.waited : stop]:
             copy.wait_send()
+        self.waited = stop
 
 
 def find_index(mesh, adjacency, seams, index):
@@ -570,7 +576,7 @@
             for j in range(EDGES):
                 source, line = decode(device, j)
                 p = (source >> 4) if h == 0 else ((source >> 2) & 3)
-                index[(h * 4 + k) * 12 + j] = (p * 4 + (source & 3)) * EDGES + line
+                index[(h * 4 + k) * 12 + j] = ((source & 1) * 8 + ((source >> 1) & 1) * 4 + p) * EDGES + line
                 if k == 0:
                     q = ((source >> 2) & 3) if h == 0 else (source >> 4)
                     index[96 + h * 12 + j] = q * EDGES + j
@@ -585,7 +591,10 @@
     chains = ((z, y, along_z, along_y), (y, z, along_y, along_z))
 
     def place(h, p, side):
-        return held[h].at[pl.ds((p * 4 + side * 2 + core) * EDGES, EDGES)]
+        return held[h].at[pl.ds((core * 8 + side * 4 + p) * EDGES, EDGES)]
+
+    def column(h, side):
+        return held[h].at[pl.ds((core * 8 + side * 4) * EDGES, 4 * EDGES)]
 
     first, over, passed, turn = [], [], [], []
     cell = ((core * 4 + y) * 4 + z) * 2
@@ -596,8 +605,8 @@
         mine = x_ref.at[pl.ds(h * EDGES, EDGES)]
         first.append([remote(mine, place(h, p, x), other) for other in others])
     for h, (p, _, _, _) in enumerate(chains):
-        over.append([remote(x_ref.at[pl.ds(h * EDGES, EDGES)], place(h, p, x), sibling)])
-        held[h][pl.ds((p * 4 + x * 2 + core) * EDGES, EDGES)] = x_ref[pl.ds(h * EDGES, EDGES)]
+        over.append([])
+        held[h][pl.ds((core * 8 + x * 4 + p) * EDGES, EDGES)] = x_ref[pl.ds(h * EDGES, EDGES)]
     cells[cell + x] = x_ref[2 * EDGES]
     yield
 
@@ -605,26 +614,23 @@
         turn[h].wait_recv()
         here = place(h, p, 1 - x)
         passed.append([remote(here, here, other) for other in others])
-        over[h].append(remote(here, here, sibling))
     cell_x.wait_recv()
     here = cells.at[pl.ds(cell, 2)]
     cell_z = [remote(here, here, other) for other in along_z]
-    for k in (0, 2, 1):
-        for h, (p, _, _, _) in enumerate(chains):
-            first[h][k].wait_recv()
-            here = place(h, (p + 3 - k) % 4, x)
-            over[h].append(remote(here, here, sibling))
+    for h in range(2):
+        for copy in first[h]:
+            copy.wait_recv()
+        over[h].append(remote(column(h, x), column(h, x), sibling))
     yield
 
     for copy in cell_z:
         copy.wait_recv()
     here = cells.at[pl.ds((core * 4 + y) * 8, 8)]
     cell_y = [remote(here, here, other) for other in along_y]
-    for k in (0, 2, 1):
-        for h, (p, _, _, _) in enumerate(chains):
-            passed[h][k].wait_recv()
-            here = place(h, (p + 3 - k) % 4, 1 - x)
-            over[h].append(remote(here, here, sibling))
+    for h in range(2):
+        for copy in passed[h]:
+            copy.wait_recv()
+        over[h].append(remote(column(h, 1 - x), column(h, 1 - x), sibling))
     yield
 
     second = []
@@ -668,23 +674,26 @@
     yield
 
 
-def total_steps(mesh, net, grads, out_grads, summed, parts, by_y, by_z):
+def total_steps(mesh, net, grads, out_grads, summed, parts, by_y, by_z, leaving):
     z, y, group, remote = mesh.z, mesh.y, mesh.group, net.send
 
     def piece(ref, g):
         return ref.at[pl.ds(pl.multiple_of(g * SHARE, 8), SHARE)]
 
+    for g in range(8):
+        leaving[g] = jnp.zeros_like(leaving[g])
+        leaving[g, :SHARE, :] = grads[pl.ds(g * SHARE, SHARE), :].astype(BF)
     scatter = [
-        remote(piece(grads, (group + k) % 8), parts.at[group], mesh.near[k - 1]) for k in range(1, 8)
+        remote(leaving.at[(group + k) % 8], parts.at[group], mesh.near[k - 1]) for k in range(1, 8)
     ]
-    parts[group] = grads[pl.ds(pl.multiple_of(group * SHARE, 8), SHARE), :]
+    parts[group] = leaving[group]
     yield
     for copy in scatter:
         copy.wait_recv()
-    total = parts[0]
+    total = parts[0].astype(F32)
     for g in range(1, 8):
-        total = total + parts[g]
-    by_y[y] = total
+        total = total + parts[g].astype(F32)
+    by_y[y] = total[:SHARE]
     add_y = [remote(by_y.at[y], by_y.at[y], other) for other in mesh.along_y]
     yield
     for copy in add_y:
@@ -695,9 +704,10 @@
     for copy in add_z:
         copy.wait_recv()
     total = ((by_z[0] + by_z[1]) + by_z[2]) + by_z[3]
-    summed[...] = total
-    out_grads[pl.ds(pl.multiple_of(group * SHARE, 8), SHARE), :] = total
-    gather = [remote(summed, piece(out_grads, group), other) for other in mesh.near]
+    summed[...] = jnp.zeros_like(summed)
+    summed[:SHARE, :] = total.astype(BF)
+    out_grads[group] = summed[...]
+    gather = [remote(summed, out_grads.at[group], other) for other in mesh.near]
     yield
     for copy in gather:
         copy.wait_recv()
@@ -714,7 +724,7 @@
     pltpu.VMEM((1024, 128), F32),
     pltpu.VMEM((1024, 128), F32),
 ]
-COPIES = 2 * (2 + 1 + 6 + 2 + 6 + 2 + 3 + 6 + 3 + 6 + 6 + 1) + 7 + 3 + 3 + 7
+COPIES = 2 * (2 + 1 + 6 + 6 + 3 + 2 + 3 + 2 + 6 + 1) + 7 + 3 + 3 + 7
 
 
 def body(fields, cotangent, first_kernel, second_kernel, adjacency, seam_codes, corner_map):
@@ -747,10 +757,12 @@
         + [w_corner] * 4
         + [turned, turned, shifted, shifted, terms, sixteen, flat, flat, flat]
         + [pltpu.VMEM((LINES + HALF, 128), F32), flat_low, flat_low, sums]
-        + [blocks, blocks, near, near, corners, corners, sums]
+        + [blocks, blocks, near, near, corners, corners, pltpu.VMEM((8, SHARE + 8, 128), BF)]
         + ROUND * 2
-        + [pltpu.VMEM((SHARE, 128), F32)]
-        + [pltpu.VMEM((k, SHARE, 128), F32) for k in (8, 4, 4)]
+        + [pltpu.VMEM((SHARE + 8, 128), BF)]
+        + [pltpu.VMEM((8, SHARE + 8, 128), BF)]
+        + [pltpu.VMEM((k, SHARE, 128), F32) for k in (4, 4)]
+        + [pltpu.VMEM((8, SHARE + 8, 128), BF)]
         + [sem((COPIES,))] * 2,
         name="whole",
         compiler_params=pltpu.CompilerParams(

time: 53.3 us -> 50.7 us (0.951)
  Pallas kernels: 52.5 us -> 49.9 us
    pallas_call x1, Pallas kernels: 50.4 us -> 47.8 us  [body(): pl.pallas_call(whole_kernel, out_shape=shapes, in_specs=[hbm] * 7, out_sp...]
where the time goes in v6:
time: 50.7 us; the launch traced here: 50.6 us
  Pallas kernels  49.9 us (98%)
  between operations  0.64 us (1%)
    pallas_call x1, Pallas kernels, body(): pl.pallas_call(whole_kernel, out_shape=shapes, in_specs=[hbm] * 7, out_sp...  47.8 us
    pallas_call x1, Pallas kernels, body(): pl.pallas_call(hand_over, out_shape=shapes, in_specs=[hbm] * 4, out_specs...  2.14 us

profile of v6, /device:TPU:1, one launch (start us, length us, event | category | flops | bytes accessed | tf_op | source)
XLA Modules:
  0.0 50.6 jit_solution(11615510317807356810)
XLA Ops:
  0.6 47.8 %whole.1 = (bf16[96,2048]{1,0:T(8,128)(2,1)}, bf16[96,2048]{1,0:T(8,128)(2,1)}, f32[576,64]{1,0:T(8,128)}, f32[576,64]{1,0:T(8,128)}) custom-call(bf16[96,2048]{1,0:T(8,128)(2,1)} %bitcast.9, bf16[96,2048]{1,0:T(8,128)(2,1)} %bitcast.10, f32[3,3,64,64]{3,2,1,0:T(8,128)} %w1_hbm.1, f32[3,3,64,64]{3,2,1,0:T(8,128)} %w2_hbm.1, s32[4,192]{1,0:T(4,128)} %bitcast.11, ...), custom_call_target="tpu_custom_call" | custom-call | tf_op jit(solution)/shard_map/whole/pallas_call | solution.py:748
  48.4 2.1 %hand_over.1 = (bf16[96,2048]{1,0:T(8,128)(2,1)}, bf16[96,2048]{1,0:T(8,128)(2,1)}, f32[576,64]{1,0:T(8,128)}, f32[576,64]{1,0:T(8,128)}) custom-call(bf16[96,2048]{1,0:T(8,128)(2,1)} %get-tuple-element.12.refs_0_, bf16[96,2048]{1,0:T(8,128)(2,1)} %get-tuple-element.13.refs_1_, f32[576,64]{1,0:T(8,128)} %get-tuple-element.14.refs_2_, ...), custom_call_target="tpu_custom_call" | custom-call | tf_op jit(solution)/shard_map/hand_over/pallas_call | solution.py:772

commit v7 on v6

--- a/solution.py
+++ b/solution.py
@@ -455,8 +455,8 @@
     next(adding)
     next(second)
     put_back(main, conv(xp, w_forth_two))
+    next(adding)
     next(second)
-    next(adding)
     fill_flat(pad_c, back, False)
     make_shifts(qp, pad_c)
     put_back(back, conv(qp, w_back_two))

time: 50.7 us -> 49.5 us (0.976)
  Pallas kernels: 49.9 us -> 48.7 us
    pallas_call x1, Pallas kernels: 47.8 us -> 46.5 us  [body(): pl.pallas_call(whole_kernel, out_shape=shapes, in_specs=[hbm] * 7, out_sp...]
where the time goes in v7:
time: 49.5 us; the launch traced here: 49.3 us
  Pallas kernels  48.7 us (98%)
  between operations  0.64 us (1%)
    pallas_call x1, Pallas kernels, body(): pl.pallas_call(whole_kernel, out_shape=shapes, in_specs=[hbm] * 7, out_sp...  46.5 us
    pallas_call x1, Pallas kernels, body(): pl.pallas_call(hand_over, out_shape=shapes, in_specs=[hbm] * 4, out_specs...  2.14 us

profile of v7, /device:TPU:1, one launch (start us, length us, event | category | flops | bytes accessed | tf_op | source)
XLA Modules:
  0.0 49.3 jit_solution(5753612291605616686)
XLA Ops:
  0.6 46.5 %whole.1 = (bf16[96,2048]{1,0:T(8,128)(2,1)}, bf16[96,2048]{1,0:T(8,128)(2,1)}, f32[576,64]{1,0:T(8,128)}, f32[576,64]{1,0:T(8,128)}) custom-call(bf16[96,2048]{1,0:T(8,128)(2,1)} %bitcast.9, bf16[96,2048]{1,0:T(8,128)(2,1)} %bitcast.10, f32[3,3,64,64]{3,2,1,0:T(8,128)} %w1_hbm.1, f32[3,3,64,64]{3,2,1,0:T(8,128)} %w2_hbm.1, s32[4,192]{1,0:T(4,128)} %bitcast.11, ...), custom_call_target="tpu_custom_call" | custom-call | tf_op jit(solution)/shard_map/whole/pallas_call | solution.py:748
  47.2 2.1 %hand_over.1 = (bf16[96,2048]{1,0:T(8,128)(2,1)}, bf16[96,2048]{1,0:T(8,128)(2,1)}, f32[576,64]{1,0:T(8,128)}, f32[576,64]{1,0:T(8,128)}) custom-call(bf16[96,2048]{1,0:T(8,128)(2,1)} %get-tuple-element.12.refs_0_, bf16[96,2048]{1,0:T(8,128)(2,1)} %get-tuple-element.13.refs_1_, f32[576,64]{1,0:T(8,128)} %get-tuple-element.14.refs_2_, ...), custom_call_target="tpu_custom_call" | custom-call | tf_op jit(solution)/shard_map/hand_over/pallas_call | solution.py:772

commit v8 on v7

--- a/solution.py
+++ b/solution.py
@@ -450,9 +450,9 @@
     adding = total_steps(mesh, net, grad, out_grads, summed, parts, by_y, by_z, leaving)
     next(adding)
     next(second)
+    next(adding)
     fill_flat(pad_f, hid, True)
     make_shifts(xp, pad_f)
-    next(adding)
     next(second)
     put_back(main, conv(xp, w_forth_two))
     next(adding)
@@ -680,9 +680,9 @@
     def piece(ref, g):
         return ref.at[pl.ds(pl.multiple_of(g * SHARE, 8), SHARE)]
 
+    fill = jnp.zeros((8, 128), F32)
     for g in range(8):
-        leaving[g] = jnp.zeros_like(leaving[g])
-        leaving[g, :SHARE, :] = grads[pl.ds(g * SHARE, SHARE), :].astype(BF)
+        leaving[g] = jnp.concatenate([grads[pl.ds(g * SHARE, SHARE), :], fill], axis=0).astype(BF)
     scatter = [
         remote(leaving.at[(group + k) % 8], parts.at[group], mesh.near[k - 1]) for k in range(1, 8)
     ]
@@ -704,8 +704,7 @@
     for copy in add_z:
         copy.wait_recv()
     total = ((by_z[0] + by_z[1]) + by_z[2]) + by_z[3]
-    summed[...] = jnp.zeros_like(summed)
-    summed[:SHARE, :] = total.astype(BF)
+    summed[...] = jnp.concatenate([total, fill], axis=0).astype(BF)
     out_grads[group] = summed[...]
     gather = [remote(summed, out_grads.at[group], other) for other in mesh.near]
     yield

time: 49.5 us -> 49.5 us (level)
  no operation moved by 1% of the time
where the time goes in v8:
time: 49.5 us; the launch traced here: 49.3 us
  Pallas kernels  48.7 us (98%)
  between operations  0.64 us (1%)
    pallas_call x1, Pallas kernels, body(): pl.pallas_call(whole_kernel, out_shape=shapes, in_specs=[hbm] * 7, out_sp...  46.5 us
    pallas_call x1, Pallas kernels, body(): pl.pallas_call(hand_over, out_shape=shapes, in_specs=[hbm] * 4, out_specs...  2.14 us

profile of v8, /device:TPU:1, one launch (start us, length us, event | category | flops | bytes accessed | tf_op | source)
XLA Modules:
  0.0 49.3 jit_solution(17898565201572636943)
XLA Ops:
  0.6 46.5 %whole.1 = (bf16[96,2048]{1,0:T(8,128)(2,1)}, bf16[96,2048]{1,0:T(8,128)(2,1)}, f32[576,64]{1,0:T(8,128)}, f32[576,64]{1,0:T(8,128)}) custom-call(bf16[96,2048]{1,0:T(8,128)(2,1)} %bitcast.9, bf16[96,2048]{1,0:T(8,128)(2,1)} %bitcast.10, f32[3,3,64,64]{3,2,1,0:T(8,128)} %w1_hbm.1, f32[3,3,64,64]{3,2,1,0:T(8,128)} %w2_hbm.1, s32[4,192]{1,0:T(4,128)} %bitcast.11, ...), custom_call_target="tpu_custom_call" | custom-call | tf_op jit(solution)/shard_map/whole/pallas_call | solution.py:747
  47.2 2.1 %hand_over.1 = (bf16[96,2048]{1,0:T(8,128)(2,1)}, bf16[96,2048]{1,0:T(8,128)(2,1)}, f32[576,64]{1,0:T(8,128)}, f32[576,64]{1,0:T(8,128)}) custom-call(bf16[96,2048]{1,0:T(8,128)(2,1)} %get-tuple-element.12.refs_0_, bf16[96,2048]{1,0:T(8,128)(2,1)} %get-tuple-element.13.refs_1_, f32[576,64]{1,0:T(8,128)} %get-tuple-element.14.refs_2_, ...), custom_call_target="tpu_custom_call" | custom-call | tf_op jit(solution)/shard_map/hand_over/pallas_call | solution.py:771
